TPU v7x, 512 devices: a whole 4x4x16 slice. The times are simulated.
512 devices in a mesh: dp: 64 (over x, z), grp: 8 (over y, core).
Axes of the slice: x: 4, y: 4, z: 16, core: 2. Of those that a mesh axis runs over, the one named last changes fastest.
Arguments:
- embeddings: bfloat16 [65536, 768], P(('dp', 'grp')), may hold values from -6 to 6
- cluster: int32 [65536, 1], P(('dp', 'grp')), may hold values from 0 to 63; in each aligned block of 128 rows (0 to 127, 128 to 255, ...) at most 4 rows name the same one
- rank: int32 [65536], P(('dp', 'grp')), may hold values from 0 to 65535, each once
Outputs:
- best_cosine: float32 [65536], P(('dp', 'grp'))
Inputs may be any that keep to these rules, and one draw needn't show every extreme that they name: Among the rows of one device, no cluster is named by more than 4 rows, a bound that some block reaches. `rank`: each number appears once.
All inputs are finite; a program needn't handle non-finite values.
Results may differ from a plain program's by a relative error of at most 0.0014.
Values may be sent and summed in bfloat16 or wider, within the bound.
A program may use at most 64 MiB of HBM per device.

v0:
```python
import jax
import jax.numpy as jnp
from jax import lax
from jax.sharding import PartitionSpec as P


def fold_block(best, queries, query_rank, keys, key_rank):
    cosine = lax.dot_general(
        queries, keys, (((1,), (1,)), ((), ())), preferred_element_type=jnp.float32
    )
    masked = jnp.where(key_rank[None, :] < query_rank[:, None], cosine, -jnp.inf)
    return jnp.maximum(best, jnp.max(masked, axis=1))


def guarded_block(best, queries, query_rank, keys, key_rank):
    return fold_block(best, queries, query_rank, keys, key_rank)


def body(embeddings, cluster, rank):
    width = embeddings.shape[1]
    rows_dev = embeddings.shape[0]
    groups = lax.axis_size("dp")
    most = 2 * rows_dev // groups
    labels = cluster[:, 0]
    values = embeddings.astype(jnp.float32)
    scale = lax.rsqrt(jnp.mean(values * values, axis=1, keepdims=True) + 1e-06) / jnp.sqrt(
        jnp.float32(width)
    )
    unit = (values * scale).astype(jnp.bfloat16)
    onehot = (labels[:, None] == jnp.arange(groups, dtype=jnp.int32)[None, :]).astype(jnp.int32)
    slot_index = jnp.sum(jnp.cumsum(onehot, axis=0) * onehot, axis=1) - 1
    position = labels * most + slot_index
    send_rows = (
        jnp.zeros((groups * most, width), jnp.bfloat16)
        .at[position]
        .set(unit)
        .reshape(groups, most, width)
    )
    send_rank = (
        jnp.full((groups * most,), 2**30, jnp.int32).at[position].set(rank).reshape(groups, most)
    )
    initial = jnp.full((groups * most,), -1.0, jnp.float32)
    recv_rows, recv_rank = (
        lax.all_to_all(send_rows, "dp", split_axis=0, concat_axis=0, tiled=True),
        lax.all_to_all(send_rank, "dp", split_axis=0, concat_axis=0, tiled=True),
    )
    queries = recv_rows.reshape(groups * most, width)
    query_rank = recv_rank.reshape(groups * most)
    best = guarded_block(
        initial,
        queries,
        query_rank,
        lax.all_gather(queries, "grp", axis=0, tiled=True),
        lax.all_gather(query_rank, "grp", axis=0, tiled=True),
    )
    returned = lax.all_to_all(
        best.reshape(groups, most), "dp", split_axis=0, concat_axis=0, tiled=True
    )
    return returned.reshape(groups * most)[position]


def solution(mesh):
    in_specs = (P(("dp", "grp"), None), P(("dp", "grp"), None), P(("dp", "grp")))
    out_specs = P(("dp", "grp"))
    return jax.shard_map(body, mesh=mesh, in_specs=in_specs, out_specs=out_specs, check_vma=False)
```

profile of v0, /device:TPU:1, one launch (start us, length us, event | category | flops | bytes accessed | tf_op | source)
XLA Modules:
  0.0 129.2 jit_solution(17333318331494720587)
XLA Ops:
  6.5 0.0 all-gather.3.cloned.1.call-start
  6.5 1.0 fusion.1
  7.6 0.7 fusion.7
  8.3 0.2 reduce_window_sum.11
  8.5 0.8 select_reduce_fusion
  9.3 0.7 fusion.8
  10.0 1.7 %scatter_custom_fusion.1 = bf16[256,768]{1,0:T(8,128)(2,1)S(1)} fusion(s32[128]{0:T(128)S(1)} %fusion.8, bf16[128,768]{1,0:T(8,128)(2,1)} %param.3, f32[128]{0:T(128)S(1)} %rsqrt_multiply_fusion, bf16[]{:T(256)} %constant.9.clone.1), kind=kCustom, calls=%fused_computation.9 | custom fusion | flops 294912 | bytes 590338 | tf_op jit(solution)/shard_map/scatter | solution.py:36
  11.7 0.1 reshape.57
  11.8 43.6 %all_to_all.20 = bf16[64,4,768]{2,1,0:T(4,128)(2,1)S(1)} all-to-all(bf16[64,4,768]{2,1,0:T(4,128)(2,1)S(1)} %reshape.57), channel_id=1, replica_groups=mesh['dp'=64,'grp'=8] {'dp'}, dimensions={0} | all-to-all | bytes 786432 | tf_op jit(solution)/shard_map/all_to_all | solution.py:44
  55.5 0.8 reshape.58
  56.3 0.0 all-gather.3.cloned.1.call-update
  56.3 1.1 scatter_custom_fusion
  57.4 0.1 all_to_all.13
  57.6 20.7 %all_to_all.21 = s32[64,1,4]{2,1,0:T(1,128)S(1)} all-to-all(s32[64,1,4]{2,1,0:T(1,128)S(1)} %bitcast.16), channel_id=1, replica_groups=mesh['dp'=64,'grp'=8] {'dp'}, dimensions={0} | all-to-all | bytes 2048 | tf_op jit(solution)/shard_map/all_to_all | solution.py:45
  78.2 0.1 reshape.56
  78.3 0.5 broadcast.72
  78.8 0.7 reduce.8
  79.6 0.1 reshape.84
  79.7 13.3 %all-gather = s32[8,1,256]{2,1,0:T(1,128)S(1)} all-gather(s32[1,1,256]{2,1,0:T(1,128)S(1)} %reshape.84), channel_id=1, replica_groups=mesh['dp'=64,'grp'=8] {'grp'}, dimensions={0}, use_global_device_ids=true | all-gather | bytes 9216 | tf_op jit(solution)/shard_map/all_gather | solution.py:54
  93.0 0.0 all-gather.3.cloned.1.call-done
  93.0 3.1 %fusion = f32[256]{0:T(256)S(1)} fusion(bf16[256,768]{1,0:T(8,128)(2,1)} %reshape.58, bf16[2048,768]{1,0:T(8,128)(2,1)} %all-gather.3.cloned.1.call-done, s32[2048]{0:T(1024)S(1)} %bitcast.17, s32[256]{0:T(256)S(1)} %reshape.56), kind=kOutput, calls=%fused_computation.4 | convolution fusion | flops 806878976 | bytes 3549184 | tf_op jit(solution)/shard_map/dot_general | solution.py:8
  96.1 0.7 max_broadcast_in_dim.15
  96.9 9.1 %all-to-all-start.2 = ((f32[64,1,4]{2,1,0:T(1,128)}), f32[64,1,4]{2,1,0:T(1,128)S(1)}, u32[]{:S(2)}, u32[]{:S(2)}) async-start(f32[64,1,4]{2,1,0:T(1,128)} %bitcast.5), calls=%async_computation.2 | async-start | bytes 65536 | tf_op jit(solution)/shard_map/all_to_all | solution.py:56
  106.0 13.3 %all-to-all-done.2 = f32[64,1,4]{2,1,0:T(1,128)S(1)} async-done(((f32[64,1,4]{2,1,0:T(1,128)}), f32[64,1,4]{2,1,0:T(1,128)S(1)}, u32[]{:S(2)}, u32[]{:S(2)}) %all-to-all-start.2) | async-done | bytes 1056 | tf_op jit(solution)/shard_map/all_to_all | solution.py:56
  119.3 0.5 broadcast.73
  119.8 0.7 reduce.9
  120.5 0.1 reshape.59
  120.6 1.8 %gather_fusion = f32[128]{0:T(128)} fusion(f32[256]{0:T(256)S(1)} %reshape.59, s32[1024]{0:T(1024)S(1)} %pad_clamp_fusion), kind=kCustom, calls=%fused_computation | custom fusion | bytes 1536 | tf_op jit(solution)/shard_map/gather | solution.py:59
  (3 shorter events, 0.0 us)
Async XLA Ops:
  6.5 86.5 %all-gather.3.cloned.1.call-start = ((), (), s32[]{:S(2)}) async-start(), calls=%async_computation.3 | async-start | bytes 3538944 | tf_op jit(solution)/shard_map/all_gather | solution.py:53
  96.9 22.4 %all-to-all-start.2 = ((f32[64,1,4]{2,1,0:T(1,128)}), f32[64,1,4]{2,1,0:T(1,128)S(1)}, u32[]{:S(2)}, u32[]{:S(2)}) async-start(f32[64,1,4]{2,1,0:T(1,128)} %bitcast.5), calls=%async_computation.2 | async-start | bytes 65536 | tf_op jit(solution)/shard_map/all_to_all | solution.py:56
Sparse Core Ops, SparseCore 0:
  56.4 30.2 all-gather.2
where the time goes:
time: 130 us; the launch traced here: 129 us
  blocking collectives  77.6 us (60%)
  between operations  13.5 us (10%)
  waiting for transfers between devices  13.3 us (10%)
  starting transfers between devices  9.09 us (7%)
  other arithmetic  6.64 us (5%)
  local copies, waits for them, and re-layouts  5.95 us (5%)
  matrix products  3.13 us (2%)
    all_to_all x1, blocking collectives, body(): lax.all_to_all(send_rows, 'dp', split_axis=0, concat_axis=0, tiled=True)  43.6 us
    all_to_all x1, blocking collectives, body(): lax.all_to_all(send_rank, 'dp', split_axis=0, concat_axis=0, tiled=True)  20.7 us
    all_gather x1, blocking collectives, body(): lax.all_gather(query_rank, 'grp', axis=0, tiled=True)  13.3 us
    all_to_all x1, waiting for transfers between devices, body(): lax.all_to_all(best.reshape(groups, most), 'dp', split_axis=0, concat_axi...  13.3 us
    all_to_all x1, starting transfers between devices, body(): lax.all_to_all(best.reshape(groups, most), 'dp', split_axis=0, concat_axi...  9.09 us
    dot_general x1, matrix products, fold_block(): lax.dot_general(queries, keys, (((1,), (1,)), ((), ())), preferred_elemen...  3.13 us
  transfers between devices with their start and end apart: 2, of which 1 were waited for; matrix products, arithmetic and copies ran while one was open for 2% of the time, Pallas kernels for 0%

commit v1 on v0

v1 whole, which is shorter than its diff:
```python
import jax
import jax.numpy as jnp
from jax import lax
from jax.experimental import pallas as pl
from jax.experimental.pallas import tpu as pltpu
from jax.sharding import PartitionSpec as P

NX, NY, NZ = 4, 4, 16
MOST = 4
CHUNKS = 4
PER = NZ // CHUNKS
ROWS = NX * MOST
SLOTS = NZ * ROWS
EMPTY = 65536.0

OFF = [0]
for step in range(1, NZ // 2 + 1):
    OFF += [step, -step]
OFF = OFF[:NZ]

F32, BF16 = jnp.float32, jnp.bfloat16


def iota(shape, dim):
    return lax.broadcasted_iota(jnp.int32, shape, dim)


def onehot(cond):
    return jnp.where(cond, 1.0, 0.0)


def dot(a, b):
    return lax.dot_general(a, b, (((1,), (0,)), ((), ())), preferred_element_type=F32)


def kernel(emb, lab, rank, out, S, Sr, R1, Rr1, Rr2, T, K, Q2, KR, QR2, PM, PMs, BS, B0, B1, V,
           z_s, z_r, zr_s, zr_r, x_s, x_r, xr_s, xr_r, y_s, y_r, yr_s, yr_r, pm_s, pm_r, b_s, b_r, v_s, v_r):
    dp, grp = lax.axis_index("dp"), lax.axis_index("grp")
    x, z = lax.div(dp, NZ), lax.rem(dp, NZ)
    y, core = lax.div(grp, 2), lax.rem(grp, 2)
    z_at = [lax.rem(z + off + NZ, NZ) for off in OFF]
    z_from = [lax.rem(z - off + NZ, NZ) for off in OFF]
    x_at = [lax.rem(x + q, NX) for q in range(NX)]
    x_from = [lax.rem(x - q + NX, NX) for q in range(NX)]
    y_at = [lax.rem(y + q, NY) for q in range(NY)]

    def along_z(zz):
        return (x * NZ + zz, grp)

    def along_x(xx):
        return (xx * NZ + z, grp)

    def along_y(yy):
        return (dp, yy * 2 + core)

    sibling = (dp, y * 2 + 1 - core)
    mesh_id = pl.DeviceIdType.MESH
    started = []

    def send(src, dst, send_sem, recv_sem, to):
        copy = pltpu.make_async_remote_copy(
            src_ref=src, dst_ref=dst, send_sem=send_sem, recv_sem=recv_sem, device_id=to, device_id_type=mesh_id
        )
        copy.start()
        started.append(copy)
        return copy

    barrier = pltpu.get_barrier_semaphore()
    peers = [along_z(z_at[p]) for p in range(1, NZ)] + [along_x(x_at[q]) for q in range(1, NX)]
    peers += [along_y(y_at[q]) for q in range(1, NY)] + [sibling]
    for peer in peers:
        pl.semaphore_signal(barrier, inc=1, device_id=peer, device_id_type=mesh_id)

    lab_row = lab[...].astype(F32)
    i0, i1 = iota((128, 128), 0), iota((128, 128), 1)
    lab_all = jnp.broadcast_to(lab_row, (128, 128))
    lab_col = jnp.sum(jnp.where(i0 == i1, lab_all, 0.0), axis=1, keepdims=True)
    same = onehot(lab_col == lab_all)
    slot_row = jnp.sum(jnp.where(i0 < i1, same, 0.0), axis=0, keepdims=True)
    slot_col = jnp.sum(jnp.where(i1 < i0, same, 0.0), axis=1, keepdims=True)
    xg_row = jnp.floor(lab_row * (1.0 / NZ))
    zg_row = lab_row - NZ * xg_row
    xg_col = jnp.floor(lab_col * (1.0 / NZ))
    pos_row = zg_row * ROWS + xg_row * MOST + slot_row

    rank_row = rank[...].astype(F32)
    high = jnp.floor(rank_row * (1.0 / 256))
    low = rank_row - 256.0 * high
    mine = zg_row == iota((NZ, 128), 0).astype(F32)
    parts = jnp.concatenate(
        [jnp.where(mine, high, 0.0), jnp.where(mine, low, 0.0), onehot(mine)], axis=0
    ).astype(BF16)
    place = onehot(xg_col * MOST + slot_col == i1.astype(F32)).astype(BF16)
    found = dot(parts, place)
    ranks = found[:NZ] * 256.0 + found[NZ:2 * NZ] + (1.0 - found[2 * NZ:]) * EMPTY
    for i in range(NZ):
        Sr[i] = ranks[i:i + 1]

    values = emb[...].astype(F32)
    scale = lax.rsqrt(jnp.mean(values * values, axis=1, keepdims=True) + 1e-06) / jnp.sqrt(F32(values.shape[1]))
    unit = (values * scale).astype(BF16)
    spread = onehot(pos_row == iota((SLOTS, 128), 0).astype(F32)).astype(BF16)
    slots = dot(spread, unit).astype(BF16)
    for i in range(NZ):
        S[i] = slots[i * ROWS:(i + 1) * ROWS]

    pl.semaphore_wait(barrier, len(peers))

    z_copy, zr_copy = [None], [None]
    for p in range(1, NZ):
        zr_copy.append(send(Sr.at[z_at[p]], Rr1.at[p], zr_s.at[p], zr_r.at[p], along_z(z_at[p])))
    for p in range(1, NZ):
        z_copy.append(send(S.at[z_at[p]], R1.at[p], z_s.at[p], z_r.at[p], along_z(z_at[p])))
    Rr1[0] = Sr[z]
    R1[0] = S[z]

    for p in range(1, NZ):
        zr_copy[p].wait_recv()
    xr_copy = [None]
    for q in range(1, NX):
        xr_copy.append(send(Rr1, Rr2.at[q], xr_s.at[q], xr_r.at[q], along_x(x_at[q])))
    Rr2[0] = Rr1[...]
    for q in range(1, NX):
        xr_copy[q].wait_recv()
    lanes = Rr2[...].reshape(NX * NZ, 128)
    lane_high = jnp.floor(lanes * (1.0 / 256))
    lane_low = lanes - 256.0 * lane_high
    r0, r1 = iota((SLOTS, NX * NZ), 0), iota((SLOTS, NX * NZ), 1)
    chunk_of, q_of, place_of = r0 // (ROWS * PER), (r0 // ROWS) % NX, (r0 // MOST) % PER
    pick = onehot(r1 == q_of * NZ + chunk_of * PER + place_of).astype(BF16)
    both = dot(pick, jnp.concatenate([lane_high, lane_low], axis=1).astype(BF16))
    wide = both[:, :128] * 256.0 + both[:, 128:]
    w0, w1 = iota((SLOTS, 128), 0), iota((SLOTS, 128), 1)
    own_col = jnp.sum(jnp.where(w1 == x * MOST + w0 % MOST, wide, 0.0), axis=1, keepdims=True)
    d0, d1 = iota((SLOTS, SLOTS), 0), iota((SLOTS, SLOTS), 1)
    KR[0] = jnp.sum(jnp.where(d0 == d1, own_col, 0.0), axis=0, keepdims=True)
    yr_copy = [None]
    for q in range(1, NY):
        yr_copy.append(send(KR.at[0], KR.at[NY - q], yr_s.at[q], yr_r.at[q], along_y(y_at[q])))
    qr_copy = send(KR.at[0], QR2, yr_s.at[0], yr_r.at[0], sibling)

    o0, o1 = iota((PER * ROWS, PER * ROWS), 0), iota((PER * ROWS, PER * ROWS), 1)
    from_x = lax.rem(x + o0 // ROWS, NX)
    order = onehot(o1 == ((o0 // MOST) % PER) * ROWS + from_x * MOST + o0 % MOST).astype(BF16)
    up, down = along_y(y_at[1]), along_y(y_at[NY - 1])
    for t in range(CHUNKS):
        for p in range(t * PER, (t + 1) * PER):
            if p:
                z_copy[p].wait_recv()
        rows = R1[t * PER:(t + 1) * PER].reshape(PER * ROWS, R1.shape[2])
        turned = dot(order, rows).astype(BF16)
        x_copy = []
        for q in range(1, NX):
            T[t, q] = turned[q * ROWS:(q + 1) * ROWS]
            x_copy.append(send(T.at[t, q], K.at[0, t, q], x_s.at[t, q], x_r.at[t, q], along_x(x_at[q])))
        K[0, t, 0] = turned[:ROWS]
        for copy in x_copy:
            copy.wait_recv()
        to_up = send(K.at[0, t], K.at[NY - 1, t], y_s.at[t, 0], y_r.at[t, 0], up)
        to_down = send(K.at[0, t], K.at[1, t], y_s.at[t, 1], y_r.at[t, 1], down)
        q2_copy = send(K.at[0, t], Q2.at[t], y_s.at[t, 2], y_r.at[t, 2], sibling)
        to_up.wait_recv()
        on_up = send(K.at[NY - 1, t, pl.ds(0, 2)], K.at[2, t, pl.ds(0, 2)], y_s.at[t, 3], y_r.at[t, 3], up)
        to_down.wait_recv()
        on_down = send(K.at[1, t, pl.ds(2, 2)], K.at[2, t, pl.ds(2, 2)], y_s.at[t, 4], y_r.at[t, 4], down)
        q2_copy.wait_recv()
        on_up.wait_recv()
        on_down.wait_recv()

    for q in range(1, NY):
        yr_copy[q].wait_recv()
    qr_copy.wait_recv()

    width = K.shape[4]
    query_rank = jnp.concatenate([KR[0], QR2[...]], axis=1)
    best = None
    for b in range(NY):
        key_rank = jnp.sum(jnp.where(d0 == d1, KR[b], 0.0), axis=1, keepdims=True)
        keys = K[b].reshape(SLOTS, width)
        halves = []
        for queries, ranks_q in ((K[0], query_rank[:, :SLOTS]), (Q2[...], query_rank[:, SLOTS:])):
            cosine = lax.dot_general(
                keys, queries.reshape(SLOTS, width), (((1,), (1,)), ((), ())), preferred_element_type=F32
            )
            masked = jnp.where(key_rank < ranks_q, cosine, -jnp.inf)
            halves.append(jnp.max(masked, axis=0, keepdims=True))
        best = halves if best is None else [jnp.maximum(a, b_) for a, b_ in zip(best, halves)]
    PMs[...] = best[1]
    pm_copy = send(PMs, PM, pm_s, pm_r, sibling)
    pm_copy.wait_recv()
    result = jnp.maximum(jnp.maximum(best[0], PM[...]), -1.0)

    BS[0:1] = result[:, :128]
    BS[1:2] = result[:, 128:]
    b_copy = []
    for q in range(1, NX):
        b_copy.append(send(BS, B0.at[q], b_s.at[q], b_r.at[q], along_x(x_from[q])))
    B0[0] = BS[...]
    for copy in b_copy:
        copy.wait_recv()
    for q in range(NX):
        for h in range(2):
            B1[h, q:q + 1] = B0[q, h:h + 1]
    v_copy = []
    for p in range(1, NZ):
        v_copy.append(send(B1.at[p // 8], V.at[p], v_s.at[p], v_r.at[p], along_z(z_from[p])))
    V[0] = B1[0]
    for copy in v_copy:
        copy.wait_recv()
    back = V[...].reshape(NZ * NX, 128)
    a0, a1 = iota((NZ * NX, 128), 0), iota((NZ * NX, 128), 1)
    p_of, q_at = a0 // NX, a0 % NX
    first = ((p_of // PER) % 2) * (ROWS * PER) + q_at * ROWS + (p_of % PER) * MOST
    held = jnp.where((a1 >= first) & (a1 < first + MOST), back, 0.0)
    shift = 64
    while shift >= MOST:
        held = held + pltpu.roll(held, shift, 1)
        shift //= 2
    off = jnp.where(p_of % 2 == 1, (p_of + 1) // 2, -(p_of // 2))
    cluster_of = (lax.rem(x + q_at, NX) * NZ + lax.rem(z + off + NZ, NZ)).astype(F32)
    chosen = jnp.zeros((NZ * NX, 128), F32)
    for s in range(MOST):
        hit = (cluster_of == lab_row) & (slot_row == float(s))
        chosen = chosen + jnp.where(hit, held[:, s:s + 1], 0.0)
    out[...] = jnp.sum(chosen, axis=0, keepdims=True)

    for copy in started:
        copy.wait_send()


def body(embeddings, cluster, rank):
    width = embeddings.shape[1]
    vmem = pl.BlockSpec(memory_space=pltpu.VMEM)
    sem = pltpu.SemaphoreType.DMA
    out = pl.pallas_call(
        kernel,
        out_shape=jax.ShapeDtypeStruct((1, 128), F32),
        in_specs=[vmem] * 3,
        out_specs=vmem,
        scratch_shapes=[
            pltpu.VMEM((NZ, ROWS, width), BF16),
            pltpu.VMEM((NZ, 1, 128), F32),
            pltpu.VMEM((NZ, ROWS, width), BF16),
            pltpu.VMEM((NZ, 1, 128), F32),
            pltpu.VMEM((NX, NZ, 1, 128), F32),
            pltpu.VMEM((CHUNKS, NX, ROWS, width), BF16),
            pltpu.VMEM((NY, CHUNKS, NX, ROWS, width), BF16),
            pltpu.VMEM((CHUNKS, NX, ROWS, width), BF16),
            pltpu.VMEM((NY, 1, SLOTS), F32),
            pltpu.VMEM((1, SLOTS), F32),
            pltpu.VMEM((1, SLOTS), F32),
            pltpu.VMEM((1, SLOTS), F32),
            pltpu.VMEM((2, 128), F32),
            pltpu.VMEM((NX, 2, 128), F32),
            pltpu.VMEM((2, NX, 128), F32),
            pltpu.VMEM((NZ, NX, 128), F32),
            sem((NZ,)), sem((NZ,)), sem((NZ,)), sem((NZ,)),
            sem((CHUNKS, NX)), sem((CHUNKS, NX)), sem((NX,)), sem((NX,)),
            sem((CHUNKS, 5)), sem((CHUNKS, 5)), sem((NY,)), sem((NY,)),
            sem, sem, sem((NX,)), sem((NX,)), sem((NZ,)), sem((NZ,)),
        ],
        compiler_params=pltpu.CompilerParams(
            collective_id=0, has_side_effects=True, vmem_limit_bytes=40 * 1024 * 1024
        ),
    )(embeddings, cluster.reshape(1, 128), rank.reshape(1, 128))
    return out.reshape(128)


def solution(mesh):
    in_specs = (P(("dp", "grp"), None), P(("dp", "grp"), None), P(("dp", "grp")))
    out_specs = P(("dp", "grp"))
    return jax.shard_map(body, mesh=mesh, in_specs=in_specs, out_specs=out_specs, check_vma=False)
```

time: 130 us -> 91.6 us (0.70)
  Pallas kernels: 0 us -> 87.8 us
  blocking collectives: 77.6 us -> 0 us
  between operations: 13.5 us -> 0.01 us
  waiting for transfers between devices: 13.3 us -> 0 us
  starting transfers between devices: 9.09 us -> 0 us
  other arithmetic: 6.64 us -> 0 us
  local copies, waits for them, and re-layouts: 5.95 us -> 2.11 us
  matrix products: 3.13 us -> 0 us
    pallas_call x0 -> x1, Pallas kernels: none -> 87.8 us  [body(): pl.pallas_call(kernel, out_shape=jax.ShapeDtypeStruct((1, 128), F32), in_...]
    all_to_all x2 -> x0, blocking collectives: 64.3 us -> none  [the longest x1 43.6 us: body(): lax.all_to_all(send_rows, 'dp', split_axis=0, concat_axis=0, tiled=True)]
    all_gather x1 -> x0, blocking collectives: 13.3 us -> none  [body(): lax.all_gather(query_rank, 'grp', axis=0, tiled=True)]
    all_to_all x1 -> x0, waiting for transfers between devices: 13.3 us -> none  [body(): lax.all_to_all(best.reshape(groups, most), 'dp', split_axis=0, concat_axi...]
    all_to_all x1 -> x0, starting transfers between devices: 9.09 us -> none  [body(): lax.all_to_all(best.reshape(groups, most), 'dp', split_axis=0, concat_axi...]
    dot_general x1 -> x0, matrix products: 3.13 us -> none  [fold_block(): lax.dot_general(queries, keys, (((1,), (1,)), ((), ())), preferred_elemen...]
    unnamed x1 -> x7, local copies, waits for them, and re-layouts: 0.1 us -> 2.11 us
    reduce_sum x2 -> x0, other arithmetic: 1.87 us -> none  [the longest x1 1.05 us: body(): jnp.mean(values * values, axis=1, keepdims=True) + 1e-06]
  transfers between devices with their start and end apart: 2 -> 0, of which waited for: 1 -> 0; matrix products, arithmetic and copies ran while one was open for 2% -> 0% of each run, Pallas kernels for 0% -> 0%
where the time goes in v1:
time: 91.6 us; the launch traced here: 89.9 us
  Pallas kernels  87.8 us (96%)
  local copies, waits for them, and re-layouts  2.11 us (2%)
    pallas_call x1, Pallas kernels, body(): pl.pallas_call(kernel, out_shape=jax.ShapeDtypeStruct((1, 128), F32), in_...  87.8 us
    unnamed x7, local copies, waits for them, and re-layouts  2.11 us

profile of v1, /device:TPU:1, one launch (start us, length us, event | category | flops | bytes accessed | tf_op | source)
XLA Modules:
  0.0 89.9 jit_solution(11224982700644189488)
XLA Ops:
  0.0 0.0 copy-start.1
  0.0 0.0 copy-start.2
  0.0 0.7 copy-done.1
  0.7 0.0 copy-done.2
  0.7 0.0 copy-start
  0.7 0.9 %copy-done = bf16[128,768]{1,0:T(8,128)(2,1)S(1)} copy-done((bf16[128,768]{1,0:T(8,128)(2,1)S(1)}, bf16[128,768]{1,0:T(8,128)(2,1)}, u32[]{:S(2)}) %copy-start) | copy-done | bytes 196632
  1.6 87.8 %shard_map.37 = f32[1,128]{1,0:T(1,128)S(1)} custom-call(bf16[128,768]{1,0:T(8,128)(2,1)S(1)} %copy-done, s32[1,128]{1,0:T(1,128)S(1)} %bitcast.3, s32[1,128]{1,0:T(1,128)S(1)} %bitcast.4), custom_call_target="tpu_custom_call" | custom-call | tf_op jit(solution)/shard_map/pallas_call | solution.py:235
  89.4 0.5 copy.5
Async XLA Ops:
  0.0 0.7 copy-start.1
  0.0 0.7 copy-start.2
  0.7 0.9 %copy-start = (bf16[128,768]{1,0:T(8,128)(2,1)S(1)}, bf16[128,768]{1,0:T(8,128)(2,1)}, u32[]{:S(2)}) copy-start(bf16[128,768]{1,0:T(8,128)(2,1)} %emb.1) | copy-start | bytes 589828

commit v2 on v0

v2 whole, which is shorter than its diff:
```python
import jax
import jax.numpy as jnp
from jax import lax
from jax.experimental import pallas as pl
from jax.experimental.pallas import tpu as pltpu
from jax.sharding import PartitionSpec as P

NX, NY, NZ = 4, 4, 16
GROUPS = NX * NZ
MOST = 4
SLOTS = GROUPS * MOST
CHUNKS = 4
PER = GROUPS // CHUNKS
CHUNK = PER * MOST
EMPTY = 65536.0

DZ = [8 - i // 2 if i % 2 == 0 else (i + 1) // 2 - 8 for i in range(NZ)]
DX = [2, 1, 3, 0]
PLACES = [(dx, dz) for dx in DX for dz in DZ]
LAST = GROUPS - 1

F32, BF16 = jnp.float32, jnp.bfloat16


def iota(shape, dim):
    return lax.broadcasted_iota(jnp.int32, shape, dim)


def onehot(cond):
    return jnp.where(cond, 1.0, 0.0)


def dot(a, b):
    return lax.dot_general(a, b, (((1,), (0,)), ((), ())), preferred_element_type=F32)


def kernel(emb_in, lab_in, rank_in, out, emb, lab, rank, S, Sr, R, Rr, K, Q2, KR, QR2, PM, PMs, BS, V,
           in_s, row_s, row_r, rr_s, rr_r, y_s, y_r, yr_s, yr_r, pm_s, pm_r, b_s, b_r):
    dp, grp = lax.axis_index("dp"), lax.axis_index("grp")
    x, z = lax.div(dp, NZ), lax.rem(dp, NZ)
    y, core = lax.div(grp, 2), lax.rem(grp, 2)
    z_at = {dz: lax.rem(z + (dz + NZ), NZ) for dz in range(1 - NZ // 2, NZ // 2 + 1)}
    z_from = {dz: lax.rem(z + (NZ - dz), NZ) for dz in z_at}
    x_at = [lax.rem(x + dx, NX) * NZ for dx in range(NX)]
    x_from = [lax.rem(x + (NX - dx), NX) * NZ for dx in range(NX)]
    y_at = [lax.rem(y + q, NY) for q in range(NY)]
    target = [x_at[dx] + z_at[dz] for dx, dz in PLACES]
    source = [x_from[dx] + z_from[dz] for dx, dz in PLACES]

    def along_y(q):
        return (dp, y_at[q] * 2 + core)

    sibling = (dp, y * 2 + 1 - core)
    mesh_id = pl.DeviceIdType.MESH
    started = []

    def send(src, dst, send_sem, recv_sem, to, keep=True):
        copy = pltpu.make_async_remote_copy(
            src_ref=src, dst_ref=dst, send_sem=send_sem, recv_sem=recv_sem, device_id=to, device_id_type=mesh_id
        )
        copy.start()
        if keep:
            started.append(copy)
        return copy

    def wait_all(ref, sem):
        pltpu.make_async_copy(ref, ref, sem).wait()

    barrier = pltpu.get_barrier_semaphore()
    peers = [(target[p], grp) for p in range(LAST)] + [along_y(q) for q in range(1, NY)] + [sibling]
    for peer in peers:
        pl.semaphore_signal(barrier, inc=1, device_id=peer, device_id_type=mesh_id)

    loads = [pltpu.make_async_copy(a, b, in_s.at[i]) for i, (a, b) in enumerate(
        ((lab_in, lab), (rank_in, rank), (emb_in, emb)))]
    for load in loads:
        load.start()
    loads[0].wait()
    loads[1].wait()

    lab_row = lab[...].astype(F32)
    i0, i1 = iota((128, 128), 0), iota((128, 128), 1)
    lab_all = jnp.broadcast_to(lab_row, (128, 128))
    lab_col = jnp.sum(jnp.where(i0 == i1, lab_all, 0.0), axis=1, keepdims=True)
    same = onehot(lab_col == lab_all)
    slot_row = jnp.sum(jnp.where(i0 < i1, same, 0.0), axis=0, keepdims=True)
    slot_col = jnp.sum(jnp.where(i1 < i0, same, 0.0), axis=1, keepdims=True)
    pos_row = lab_row * MOST + slot_row
    pos_col = lab_col * MOST + slot_col

    rank_row = rank[...].astype(F32)
    high = jnp.floor(rank_row * (1.0 / 256))
    low = rank_row - 256.0 * high
    half_row = jnp.floor(pos_row * (1.0 / 128))
    half_col = jnp.floor(pos_col * (1.0 / 128))
    mine = half_row == iota((8, 128), 0).astype(F32)
    parts = jnp.concatenate(
        [jnp.where(mine, high, 0.0), jnp.where(mine, low, 0.0), onehot(mine)], axis=0
    ).astype(BF16)
    place = onehot(pos_col - 128.0 * half_col == i1.astype(F32)).astype(BF16)
    found = dot(parts, place)
    ranks = found[:8] * 256.0 + found[8:16] + (1.0 - found[16:]) * EMPTY
    for i in range(2):
        Sr[i] = ranks[i:i + 1]

    width = emb.shape[1]
    half = width // 2
    s0, s1 = iota((2 * SLOTS, 256), 0), iota((2 * SLOTS, 256), 1)
    slot_of = (s0 // 8) * MOST + s0 % MOST
    pos_two = jnp.concatenate([pos_row, pos_row], axis=1)
    spread = onehot((pos_two == slot_of.astype(F32)) & ((s0 // MOST) % 2 == s1 // 128)).astype(BF16)
    loads[2].wait()
    values = emb[...].astype(F32)
    scale = lax.rsqrt(jnp.mean(values * values, axis=1, keepdims=True) + 1e-06) / jnp.sqrt(F32(width))
    unit = (values * scale).astype(BF16)
    S[...] = dot(spread, jnp.concatenate([unit[:, :half], unit[:, half:]], axis=0)).astype(BF16).reshape(S.shape)

    pl.semaphore_wait(barrier, len(peers))

    def send_rows(places):
        for p in places:
            send(S.at[target[p]], R.at[p], row_s, row_r.at[p // PER], (target[p], grp), False)

    send_rows(range(PER))
    for p in range(LAST):
        send(Sr.at[lax.div(target[p], 32)], Rr.at[p], rr_s, rr_r, (target[p], grp), False)
    send_rows(range(PER, LAST))
    R[LAST] = S[dp]
    Rr[LAST] = Sr[lax.div(dp, 32)]

    o0, o1 = iota((2 * CHUNK, 2 * CHUNK), 0), iota((2 * CHUNK, 2 * CHUNK), 1)
    whole = onehot(o1 == ((o0 % CHUNK) // MOST) * 8 + (o0 // CHUNK) * MOST + o0 % MOST).astype(BF16)
    up, down = along_y(1), along_y(NY - 1)
    from_down, from_up, q2_copy, on = {}, {}, {}, []

    def arrive(t):
        wait_all(R.at[pl.ds(t * PER, PER - (t == CHUNKS - 1))], row_r.at[t])
        rows = dot(whole, R[t * PER:(t + 1) * PER].reshape(2 * CHUNK, half)).astype(BF16)
        K[0, t, :, :half] = rows[:CHUNK]
        K[0, t, :, half:] = rows[CHUNK:]
        from_down[t] = send(K.at[0, t], K.at[NY - 1, t], y_s.at[t, 0], y_r.at[t, 0], up)
        from_up[t] = send(K.at[0, t], K.at[1, t], y_s.at[t, 1], y_r.at[t, 1], down)
        q2_copy[t] = send(K.at[0, t], Q2.at[t], y_s.at[t, 2], y_r.at[t, 2], sibling)

    def forward(t):
        a, b = pl.ds(0, CHUNK // 2), pl.ds(CHUNK // 2, CHUNK // 2)
        from_down[t].wait_recv()
        on.append(send(K.at[NY - 1, t, a], K.at[2, t, a], y_s.at[t, 3], y_r.at[t, 3], up))
        from_up[t].wait_recv()
        on.append(send(K.at[1, t, b], K.at[2, t, b], y_s.at[t, 4], y_r.at[t, 4], down))

    arrive(0)

    wait_all(Rr.at[pl.ds(0, LAST)], rr_r)
    lanes = Rr[...].reshape(GROUPS, 128)
    lane_high = jnp.floor(lanes * (1.0 / 256))
    lane_low = lanes - 256.0 * lane_high
    pick = onehot(iota((SLOTS, GROUPS), 1) == iota((SLOTS, GROUPS), 0) // MOST).astype(BF16)
    both = dot(pick, jnp.concatenate([lane_high, lane_low], axis=1).astype(BF16))
    wide = both[:, :128] * 256.0 + both[:, 128:]
    w0, w1 = iota((SLOTS, 128), 0), iota((SLOTS, 128), 1)
    own_col = jnp.sum(jnp.where(w1 == lax.rem(dp, 32) * MOST + w0 % MOST, wide, 0.0), axis=1, keepdims=True)
    d0, d1 = iota((SLOTS, SLOTS), 0), iota((SLOTS, SLOTS), 1)
    KR[0] = jnp.sum(jnp.where(d0 == d1, own_col, 0.0), axis=0, keepdims=True)
    yr_copy = [send(KR.at[0], KR.at[NY - q], yr_s.at[q], yr_r.at[q], along_y(q)) for q in range(1, NY)]
    yr_copy.append(send(KR.at[0], QR2, yr_s.at[0], yr_r.at[0], sibling))

    arrive(1)
    forward(0)
    arrive(2)
    forward(1)
    arrive(3)
    forward(2)
    forward(3)
    for copy in yr_copy + list(q2_copy.values()) + on:
        copy.wait_recv()

    query_rank = jnp.concatenate([KR[0], QR2[...]], axis=1)
    best = None
    for b in range(NY):
        key_rank = jnp.sum(jnp.where(d0 == d1, KR[b], 0.0), axis=1, keepdims=True)
        keys = K[b].reshape(SLOTS, width)
        halves = []
        for queries, ranks_q in ((K[0], query_rank[:, :SLOTS]), (Q2[...], query_rank[:, SLOTS:])):
            cosine = lax.dot_general(
                keys, queries.reshape(SLOTS, width), (((1,), (1,)), ((), ())), preferred_element_type=F32
            )
            masked = jnp.where(key_rank < ranks_q, cosine, -jnp.inf)
            halves.append(jnp.max(masked, axis=0, keepdims=True))
        best = halves if best is None else [jnp.maximum(a, b_) for a, b_ in zip(best, halves)]
    PMs[...] = best[1]
    send(PMs, PM, pm_s, pm_r, sibling).wait_recv()
    result = jnp.maximum(jnp.maximum(best[0], PM[...]), -1.0)

    BS[0] = result[:, :128]
    BS[1] = result[:, 128:]
    for p in range(LAST):
        send(BS.at[p // 32], V.at[p], b_s, b_r, (source[p], grp), False)
    V[LAST] = BS[1]
    a0, a1 = iota((GROUPS, 128), 0), iota((GROUPS, 128), 1)
    i, j = a0 % NZ, a0 // NZ
    dz = jnp.where(i % 2 == 1, (i + 1) // 2 - 8, 8 - i // 2)
    dx = jnp.where(j == 0, 2, jnp.where(j == 2, 3, 1 - j // 3))
    cluster_of = (lax.rem(x + dx, NX) * NZ + lax.rem(z + dz + NZ, NZ)).astype(F32)
    first = (a0 % 32) * MOST
    wait_all(V.at[pl.ds(0, LAST)], b_r)
    held = jnp.where((a1 >= first) & (a1 < first + MOST), V[...].reshape(GROUPS, 128), 0.0)
    shift = 64
    while shift >= MOST:
        held = held + pltpu.roll(held, shift, 1)
        shift //= 2
    chosen = jnp.zeros((GROUPS, 128), F32)
    for s in range(MOST):
        hit = (cluster_of == lab_row) & (slot_row == float(s))
        chosen = chosen + jnp.where(hit, held[:, s:s + 1], 0.0)
    out[...] = jnp.sum(chosen, axis=0, keepdims=True)

    wait_all(R.at[pl.ds(0, LAST)], row_s)
    wait_all(Rr.at[pl.ds(0, LAST)], rr_s)
    wait_all(V.at[pl.ds(0, LAST)], b_s)
    for copy in started:
        copy.wait_send()


def body(embeddings, cluster, rank):
    rows, width = embeddings.shape
    sem = pltpu.SemaphoreType.DMA
    out = pl.pallas_call(
        kernel,
        out_shape=jax.ShapeDtypeStruct((1, rows), F32),
        in_specs=[pl.BlockSpec(memory_space=pl.ANY)] * 3,
        out_specs=pl.BlockSpec(memory_space=pltpu.VMEM),
        scratch_shapes=[
            pltpu.VMEM((rows, width), BF16),
            pltpu.VMEM((1, rows), jnp.int32),
            pltpu.VMEM((1, rows), jnp.int32),
            pltpu.VMEM((GROUPS, 8, width // 2), BF16),
            pltpu.VMEM((2, 1, 128), F32),
            pltpu.VMEM((GROUPS, 8, width // 2), BF16),
            pltpu.VMEM((GROUPS, 1, 128), F32),
            pltpu.VMEM((NY, CHUNKS, CHUNK, width), BF16),
            pltpu.VMEM((CHUNKS, CHUNK, width), BF16),
            pltpu.VMEM((NY, 1, SLOTS), F32),
            pltpu.VMEM((1, SLOTS), F32),
            pltpu.VMEM((1, SLOTS), F32),
            pltpu.VMEM((1, SLOTS), F32),
            pltpu.VMEM((2, 1, 128), F32),
            pltpu.VMEM((GROUPS, 1, 128), F32),
            sem((3,)),
            sem, sem((CHUNKS,)), sem, sem,
            sem((CHUNKS, 5)), sem((CHUNKS, 5)), sem((NY,)), sem((NY,)),
            sem, sem, sem, sem,
        ],
        compiler_params=pltpu.CompilerParams(
            collective_id=0, has_side_effects=True, vmem_limit_bytes=40 * 1024 * 1024
        ),
    )(embeddings, cluster.reshape(1, rows), rank.reshape(1, rows))
    return out.reshape(rows)


def solution(mesh):
    in_specs = (P(("dp", "grp"), None), P(("dp", "grp"), None), P(("dp", "grp")))
    out_specs = P(("dp", "grp"))
    return jax.shard_map(body, mesh=mesh, in_specs=in_specs, out_specs=out_specs, check_vma=False)
```

time: 130 us -> 61.9 us (0.48)
  blocking collectives: 77.6 us -> 0 us
  Pallas kernels: 0 us -> 59.6 us
  between operations: 13.5 us -> 0.01 us
  waiting for transfers between devices: 13.3 us -> 0 us
  starting transfers between devices: 9.09 us -> 0 us
  other arithmetic: 6.64 us -> 0 us
  local copies, waits for them, and re-layouts: 5.95 us -> 2.11 us
  matrix products: 3.13 us -> 0 us
    all_to_all x2 -> x0, blocking collectives: 64.3 us -> none  [the longest x1 43.6 us: body(): lax.all_to_all(send_rows, 'dp', split_axis=0, concat_axis=0, tiled=True)]
    pallas_call x0 -> x1, Pallas kernels: none -> 59.6 us  [body(): pl.pallas_call(kernel, out_shape=jax.ShapeDtypeStruct((1, rows), F32), in...]
    all_gather x1 -> x0, blocking collectives: 13.3 us -> none  [body(): lax.all_gather(query_rank, 'grp', axis=0, tiled=True)]
    all_to_all x1 -> x0, waiting for transfers between devices: 13.3 us -> none  [body(): lax.all_to_all(best.reshape(groups, most), 'dp', split_axis=0, concat_axi...]
    all_to_all x1 -> x0, starting transfers between devices: 9.09 us -> none  [body(): lax.all_to_all(best.reshape(groups, most), 'dp', split_axis=0, concat_axi...]
    dot_general x1 -> x0, matrix products: 3.13 us -> none  [fold_block(): lax.dot_general(queries, keys, (((1,), (1,)), ((), ())), preferred_elemen...]
    unnamed x1 -> x7, local copies, waits for them, and re-layouts: 0.1 us -> 2.11 us
    reduce_sum x2 -> x0, other arithmetic: 1.87 us -> none  [the longest x1 1.05 us: body(): jnp.mean(values * values, axis=1, keepdims=True) + 1e-06]
  transfers between devices with their start and end apart: 2 -> 0, of which waited for: 1 -> 0; matrix products, arithmetic and copies ran while one was open for 2% -> 0% of each run, Pallas kernels for 0% -> 0%
where the time goes in v2:
time: 61.9 us; the launch traced here: 61.7 us
  Pallas kernels  59.6 us (96%)
  local copies, waits for them, and re-layouts  2.11 us (3%)
    pallas_call x1, Pallas kernels, body(): pl.pallas_call(kernel, out_shape=jax.ShapeDtypeStruct((1, rows), F32), in...  59.6 us
    unnamed x7, local copies, waits for them, and re-layouts  2.11 us

profile of v2, /device:TPU:1, one launch (start us, length us, event | category | flops | bytes accessed | tf_op | source)
XLA Modules:
  0.0 61.7 jit_solution(13846779637325159592)
XLA Ops:
  0.0 0.0 copy-start.1
  0.0 0.0 copy-start.2
  0.0 0.7 %copy-done.1 = s32[128,1]{0,1:T(1,128)S(1)} copy-done((s32[128,1]{0,1:T(1,128)S(1)}, s32[128,1]{0,1:T(1,128)}, u32[]{:S(2)}) %copy-start.1) | copy-done | bytes 536
  0.7 0.0 copy-done.2
  0.7 0.0 copy-start
  0.7 0.9 %copy-done = bf16[128,768]{1,0:T(8,128)(2,1)S(1)} copy-done((bf16[128,768]{1,0:T(8,128)(2,1)S(1)}, bf16[128,768]{1,0:T(8,128)(2,1)}, u32[]{:S(2)}) %copy-start) | copy-done | bytes 196632
  1.6 59.6 %shard_map.37 = f32[1,128]{1,0:T(1,128)S(1)} custom-call(bf16[128,768]{1,0:T(8,128)(2,1)S(1)} %copy-done, s32[1,128]{1,0:T(1,128)S(1)} %bitcast.3, s32[1,128]{1,0:T(1,128)S(1)} %bitcast.4), custom_call_target="tpu_custom_call" | custom-call | tf_op jit(solution)/shard_map/pallas_call | solution.py:228
  61.2 0.5 copy.5
Async XLA Ops:
  0.0 0.7 %copy-start.1 = (s32[128,1]{0,1:T(1,128)S(1)}, s32[128,1]{0,1:T(1,128)}, u32[]{:S(2)}) copy-start(s32[128,1]{0,1:T(1,128)} %param.4) | copy-start | bytes 1540
  0.0 0.7 %copy-start.2 = (s32[128]{0:T(128)S(1)}, s32[128]{0:T(128)}, u32[]{:S(2)}) copy-start(s32[128]{0:T(128)} %param.5) | copy-start | bytes 1540
  0.7 0.9 %copy-start = (bf16[128,768]{1,0:T(8,128)(2,1)S(1)}, bf16[128,768]{1,0:T(8,128)(2,1)}, u32[]{:S(2)}) copy-start(bf16[128,768]{1,0:T(8,128)(2,1)} %emb_in.1) | copy-start | bytes 589828

commit v3 on v2

--- a/solution.py
+++ b/solution.py
@@ -9,14 +9,18 @@
 GROUPS = NX * NZ
 MOST = 4
 SLOTS = GROUPS * MOST
-CHUNKS = 4
-PER = GROUPS // CHUNKS
-CHUNK = PER * MOST
 EMPTY = 65536.0
 
-DZ = [8 - i // 2 if i % 2 == 0 else (i + 1) // 2 - 8 for i in range(NZ)]
-DX = [2, 1, 3, 0]
-PLACES = [(dx, dz) for dx in DX for dz in DZ]
+REACH = 4
+NEAR = [(dx, dz) for dx in (2, 1, 3, 0) for d in range(REACH, 0, -1) for dz in (d, -d)]
+NEAR = [place for dx in (2, 1, 3, 0) for place in [n for n in NEAR if n[0] == dx] + [(dx, 0)]]
+FAR = [(dx, dz) for dx in (2, 1, 3, 0) for dz in (8, -7, 7, -6, 6, -5, 5)]
+FIRST = 28
+PLACES = NEAR[:FIRST] + FAR + NEAR[FIRST:]
+SPANS = [(0, 16), (16, 28), (28, 44), (44, 56), (56, 64)]
+CHUNKS = len(SPANS)
+RELAYED = 3
+EARLY = SPANS[RELAYED][0] * MOST
 LAST = GROUPS - 1
 
 F32, BF16 = jnp.float32, jnp.bfloat16
@@ -35,7 +39,7 @@
 
 
 def kernel(emb_in, lab_in, rank_in, out, emb, lab, rank, S, Sr, R, Rr, K, Q2, KR, QR2, PM, PMs, BS, V,
-           in_s, row_s, row_r, rr_s, rr_r, y_s, y_r, yr_s, yr_r, pm_s, pm_r, b_s, b_r):
+           gate, in_s, row_s, row_r, rr_s, rr_r, y_s, y_r, yr_s, yr_r, pm_s, pm_r, b_s, b_r):
     dp, grp = lax.axis_index("dp"), lax.axis_index("grp")
     x, z = lax.div(dp, NZ), lax.rem(dp, NZ)
     y, core = lax.div(grp, 2), lax.rem(grp, 2)
@@ -67,9 +71,20 @@
         pltpu.make_async_copy(ref, ref, sem).wait()
 
     barrier = pltpu.get_barrier_semaphore()
-    peers = [(target[p], grp) for p in range(LAST)] + [along_y(q) for q in range(1, NY)] + [sibling]
+    far = [abs(dz) > REACH for _, dz in PLACES]
+    peers = [(target[p], y * 2 + int(far[p])) for p in range(LAST)] + [along_y(q) for q in range(1, NY)] + [sibling]
     for peer in peers:
         pl.semaphore_signal(barrier, inc=1, device_id=peer, device_id_type=mesh_id)
+
+    def listen(reach, count):
+        @pl.when(core == reach)
+        def _():
+            pl.semaphore_wait(barrier, 2 * count + NY)
+            pl.semaphore_signal(gate, inc=1, device_id=sibling, device_id_type=mesh_id)
+
+        @pl.when(core != reach)
+        def _():
+            pl.semaphore_wait(gate, 1)
 
     loads = [pltpu.make_async_copy(a, b, in_s.at[i]) for i, (a, b) in enumerate(
         ((lab_in, lab), (rank_in, rank), (emb_in, emb)))]
@@ -115,41 +130,62 @@
     unit = (values * scale).astype(BF16)
     S[...] = dot(spread, jnp.concatenate([unit[:, :half], unit[:, half:]], axis=0)).astype(BF16).reshape(S.shape)
 
-    pl.semaphore_wait(barrier, len(peers))
+    chunk_of = [t for t, (lo, hi) in enumerate(SPANS) for _ in range(lo, hi)]
 
     def send_rows(places):
         for p in places:
-            send(S.at[target[p]], R.at[p], row_s, row_r.at[p // PER], (target[p], grp), False)
-
-    send_rows(range(PER))
-    for p in range(LAST):
-        send(Sr.at[lax.div(target[p], 32)], Rr.at[p], rr_s, rr_r, (target[p], grp), False)
-    send_rows(range(PER, LAST))
+            send(S.at[target[p]], R.at[p], row_s, row_r.at[chunk_of[p]], (target[p], grp), False)
+
+    def send_ranks(places):
+        for p in places:
+            send(Sr.at[lax.div(target[p], 32)], Rr.at[p], rr_s, rr_r, (target[p], grp), False)
+
+    listen(0, LAST - sum(far))
+    send_rows(range(FIRST))
+    send_ranks([p for p in range(LAST) if not far[p]])
+    listen(1, sum(far))
+    send_ranks([p for p in range(LAST) if far[p]])
+    send_rows(range(FIRST, LAST))
     R[LAST] = S[dp]
     Rr[LAST] = Sr[lax.div(dp, 32)]
 
-    o0, o1 = iota((2 * CHUNK, 2 * CHUNK), 0), iota((2 * CHUNK, 2 * CHUNK), 1)
-    whole = onehot(o1 == ((o0 % CHUNK) // MOST) * 8 + (o0 // CHUNK) * MOST + o0 % MOST).astype(BF16)
-    up, down = along_y(1), along_y(NY - 1)
-    from_down, from_up, q2_copy, on = {}, {}, {}, []
+    up, across, down = along_y(1), along_y(2), along_y(NY - 1)
+    from_down, from_up, rest = {}, {}, {t: [] for t in range(CHUNKS)}
+
+    def span(t):
+        lo, hi = SPANS[t]
+        return lo, hi - lo, pl.ds(lo * MOST, (hi - lo) * MOST)
 
     def arrive(t):
-        wait_all(R.at[pl.ds(t * PER, PER - (t == CHUNKS - 1))], row_r.at[t])
-        rows = dot(whole, R[t * PER:(t + 1) * PER].reshape(2 * CHUNK, half)).astype(BF16)
-        K[0, t, :, :half] = rows[:CHUNK]
-        K[0, t, :, half:] = rows[CHUNK:]
-        from_down[t] = send(K.at[0, t], K.at[NY - 1, t], y_s.at[t, 0], y_r.at[t, 0], up)
-        from_up[t] = send(K.at[0, t], K.at[1, t], y_s.at[t, 1], y_r.at[t, 1], down)
-        q2_copy[t] = send(K.at[0, t], Q2.at[t], y_s.at[t, 2], y_r.at[t, 2], sibling)
+        lo, places, at = span(t)
+        wait_all(R.at[pl.ds(lo, places - (t == CHUNKS - 1))], row_r.at[t])
+        count = places * MOST
+        o0, o1 = iota((2 * count, 2 * count), 0), iota((2 * count, 2 * count), 1)
+        whole = onehot(o1 == ((o0 % count) // MOST) * 8 + (o0 // count) * MOST + o0 % MOST).astype(BF16)
+        rows = dot(whole, R[lo:lo + places].reshape(2 * count, half)).astype(BF16)
+        K[0, lo * MOST:lo * MOST + count, :half] = rows[:count]
+        K[0, lo * MOST:lo * MOST + count, half:] = rows[count:]
+        from_down[t] = send(K.at[0, at], K.at[3, at], y_s.at[t, 0], y_r.at[t, 0], up)
+        from_up[t] = send(K.at[0, at], K.at[1, at], y_s.at[t, 1], y_r.at[t, 1], down)
+        rest[t].append(send(K.at[0, at], Q2.at[at], y_s.at[t, 2], y_r.at[t, 2], sibling))
+        if t >= RELAYED:
+            rest[t].append(send(K.at[0, at], K.at[2, at], y_s.at[t, 3], y_r.at[t, 3], across))
+            rest[t] += [from_down[t], from_up[t]]
 
     def forward(t):
-        a, b = pl.ds(0, CHUNK // 2), pl.ds(CHUNK // 2, CHUNK // 2)
+        lo, places, _ = span(t)
+        some = places // 8 * 16
+        a, b = pl.ds(lo * MOST, some), pl.ds(lo * MOST + some, places * MOST - some)
         from_down[t].wait_recv()
-        on.append(send(K.at[NY - 1, t, a], K.at[2, t, a], y_s.at[t, 3], y_r.at[t, 3], up))
+        rest[t].append(send(K.at[3, a], K.at[2, a], y_s.at[t, 3], y_r.at[t, 3], up))
         from_up[t].wait_recv()
-        on.append(send(K.at[1, t, b], K.at[2, t, b], y_s.at[t, 4], y_r.at[t, 4], down))
+        rest[t].append(send(K.at[1, b], K.at[2, b], y_s.at[t, 4], y_r.at[t, 4], down))
 
     arrive(0)
+    arrive(1)
+    forward(0)
+    arrive(2)
+    forward(1)
 
     wait_all(Rr.at[pl.ds(0, LAST)], rr_r)
     lanes = Rr[...].reshape(GROUPS, 128)
@@ -165,43 +201,56 @@
     yr_copy = [send(KR.at[0], KR.at[NY - q], yr_s.at[q], yr_r.at[q], along_y(q)) for q in range(1, NY)]
     yr_copy.append(send(KR.at[0], QR2, yr_s.at[0], yr_r.at[0], sibling))
 
-    arrive(1)
-    forward(0)
-    arrive(2)
-    forward(1)
     arrive(3)
     forward(2)
-    forward(3)
-    for copy in yr_copy + list(q2_copy.values()) + on:
+    arrive(4)
+
+    rows8 = iota((8, 128), 0)
+    cluster_of = []
+    for p in range(0, GROUPS, 8):
+        block = jnp.zeros((8, 128), jnp.int32)
+        for i in range(8):
+            block = jnp.where(rows8 == i, target[p + i] if p + i < LAST else dp, block)
+        cluster_of.append(block)
+    cluster_of = jnp.concatenate(cluster_of, axis=0).astype(F32)
+
+    def cosines(best, keys, key_rank, queries, ranks_q):
+        cosine = lax.dot_general(keys, queries, (((1,), (1,)), ((), ())), preferred_element_type=F32)
+        masked = jnp.where(key_rank < ranks_q, cosine, -jnp.inf)
+        return jnp.maximum(best, jnp.max(masked, axis=0, keepdims=True))
+
+    for copy in yr_copy:
         copy.wait_recv()
-
-    query_rank = jnp.concatenate([KR[0], QR2[...]], axis=1)
-    best = None
+    query_rank = [KR[0], QR2[...]]
+    key_rank = [jnp.sum(jnp.where(d0 == d1, KR[b], 0.0), axis=1, keepdims=True) for b in range(NY)]
+    for t in range(RELAYED):
+        for copy in rest[t]:
+            copy.wait_recv()
+    early = [jnp.full((1, EARLY), -1.0, F32)] * 2
     for b in range(NY):
-        key_rank = jnp.sum(jnp.where(d0 == d1, KR[b], 0.0), axis=1, keepdims=True)
-        keys = K[b].reshape(SLOTS, width)
-        halves = []
-        for queries, ranks_q in ((K[0], query_rank[:, :SLOTS]), (Q2[...], query_rank[:, SLOTS:])):
-            cosine = lax.dot_general(
-                keys, queries.reshape(SLOTS, width), (((1,), (1,)), ((), ())), preferred_element_type=F32
-            )
-            masked = jnp.where(key_rank < ranks_q, cosine, -jnp.inf)
-            halves.append(jnp.max(masked, axis=0, keepdims=True))
-        best = halves if best is None else [jnp.maximum(a, b_) for a, b_ in zip(best, halves)]
+        for c, queries in enumerate((K[0, :EARLY], Q2[:EARLY])):
+            early[c] = cosines(early[c], K[b, :EARLY], key_rank[b][:EARLY], queries, query_rank[c][:, :EARLY])
+    for t in range(RELAYED, CHUNKS):
+        for copy in rest[t]:
+            copy.wait_recv()
+    late = [jnp.full((1, SLOTS - EARLY), -1.0, F32)] * 2
+    best = [jnp.full((1, SLOTS), -1.0, F32)] * 2
+    for b in range(NY):
+        for c, queries in enumerate((K.at[0], Q2)):
+            late[c] = cosines(late[c], K[b, :EARLY], key_rank[b][:EARLY], queries[EARLY:], query_rank[c][:, EARLY:])
+            best[c] = cosines(best[c], K[b, EARLY:], key_rank[b][EARLY:], queries[...], query_rank[c])
+    best = [jnp.maximum(best[c], jnp.concatenate([early[c], late[c]], axis=1)) for c in range(2)]
     PMs[...] = best[1]
     send(PMs, PM, pm_s, pm_r, sibling).wait_recv()
-    result = jnp.maximum(jnp.maximum(best[0], PM[...]), -1.0)
+    result = jnp.maximum(best[0], PM[...])
 
     BS[0] = result[:, :128]
     BS[1] = result[:, 128:]
-    for p in range(LAST):
+    hops = [min(dx, NX - dx) + abs(dz) for dx, dz in PLACES]
+    for p in sorted(range(LAST), key=lambda p: -hops[p]):
         send(BS.at[p // 32], V.at[p], b_s, b_r, (source[p], grp), False)
     V[LAST] = BS[1]
     a0, a1 = iota((GROUPS, 128), 0), iota((GROUPS, 128), 1)
-    i, j = a0 % NZ, a0 // NZ
-    dz = jnp.where(i % 2 == 1, (i + 1) // 2 - 8, 8 - i // 2)
-    dx = jnp.where(j == 0, 2, jnp.where(j == 2, 3, 1 - j // 3))
-    cluster_of = (lax.rem(x + dx, NX) * NZ + lax.rem(z + dz + NZ, NZ)).astype(F32)
     first = (a0 % 32) * MOST
     wait_all(V.at[pl.ds(0, LAST)], b_r)
     held = jnp.where((a1 >= first) & (a1 < first + MOST), V[...].reshape(GROUPS, 128), 0.0)
@@ -238,14 +287,15 @@
             pltpu.VMEM((2, 1, 128), F32),
             pltpu.VMEM((GROUPS, 8, width // 2), BF16),
             pltpu.VMEM((GROUPS, 1, 128), F32),
-            pltpu.VMEM((NY, CHUNKS, CHUNK, width), BF16),
-            pltpu.VMEM((CHUNKS, CHUNK, width), BF16),
+            pltpu.VMEM((NY, SLOTS, width), BF16),
+            pltpu.VMEM((SLOTS, width), BF16),
             pltpu.VMEM((NY, 1, SLOTS), F32),
             pltpu.VMEM((1, SLOTS), F32),
             pltpu.VMEM((1, SLOTS), F32),
             pltpu.VMEM((1, SLOTS), F32),
             pltpu.VMEM((2, 1, 128), F32),
             pltpu.VMEM((GROUPS, 1, 128), F32),
+            pltpu.SemaphoreType.REGULAR,
             sem((3,)),
             sem, sem((CHUNKS,)), sem, sem,
             sem((CHUNKS, 5)), sem((CHUNKS, 5)), sem((NY,)), sem((NY,)),

time: 61.9 us -> 61.5 us (level)
  no operation moved by 1% of the time
where the time goes in v3:
time: 61.5 us; the launch traced here: 61.3 us
  Pallas kernels  59.2 us (96%)
  local copies, waits for them, and re-layouts  2.11 us (3%)
    pallas_call x1, Pallas kernels, body(): pl.pallas_call(kernel, out_shape=jax.ShapeDtypeStruct((1, rows), F32), in...  59.2 us
    unnamed x7, local copies, waits for them, and re-layouts  2.11 us

profile of v3, /device:TPU:1, one launch (start us, length us, event | category | flops | bytes accessed | tf_op | source)
XLA Modules:
  0.0 61.3 jit_solution(14835562528124490721)
XLA Ops:
  0.0 0.0 copy-start.1
  0.0 0.0 copy-start.2
  0.0 0.7 %copy-done.1 = s32[128,1]{0,1:T(1,128)S(1)} copy-done((s32[128,1]{0,1:T(1,128)S(1)}, s32[128,1]{0,1:T(1,128)}, u32[]{:S(2)}) %copy-start.1) | copy-done | bytes 536
  0.7 0.0 copy-done.2
  0.7 0.0 copy-start
  0.7 0.9 %copy-done = bf16[128,768]{1,0:T(8,128)(2,1)S(1)} copy-done((bf16[128,768]{1,0:T(8,128)(2,1)S(1)}, bf16[128,768]{1,0:T(8,128)(2,1)}, u32[]{:S(2)}) %copy-start) | copy-done | bytes 196632
  1.6 59.2 %shard_map.37 = f32[1,128]{1,0:T(1,128)S(1)} custom-call(bf16[128,768]{1,0:T(8,128)(2,1)S(1)} %copy-done, s32[1,128]{1,0:T(1,128)S(1)} %bitcast.3, s32[1,128]{1,0:T(1,128)S(1)} %bitcast.4), custom_call_target="tpu_custom_call" | custom-call | tf_op jit(solution)/shard_map/pallas_call | solution.py:277
  60.8 0.5 copy.5
Async XLA Ops:
  0.0 0.7 %copy-start.1 = (s32[128,1]{0,1:T(1,128)S(1)}, s32[128,1]{0,1:T(1,128)}, u32[]{:S(2)}) copy-start(s32[128,1]{0,1:T(1,128)} %param.4) | copy-start | bytes 1540
  0.0 0.7 %copy-start.2 = (s32[128]{0:T(128)S(1)}, s32[128]{0:T(128)}, u32[]{:S(2)}) copy-start(s32[128]{0:T(128)} %param.5) | copy-start | bytes 1540
  0.7 0.9 %copy-start = (bf16[128,768]{1,0:T(8,128)(2,1)S(1)}, bf16[128,768]{1,0:T(8,128)(2,1)}, u32[]{:S(2)}) copy-start(bf16[128,768]{1,0:T(8,128)(2,1)} %emb_in.1) | copy-start | bytes 589828

commit v4 on v3

v4 whole, which is shorter than its diff:
```python
import jax
import jax.numpy as jnp
from jax import lax
from jax.experimental import pallas as pl
from jax.experimental.pallas import tpu as pltpu
from jax.sharding import PartitionSpec as P

NX, NY, NZ = 4, 4, 16
GROUPS = NX * NZ
MOST = 4
SLOTS = GROUPS * MOST
EMPTY = 65536.0

REACH = 4
NEAR = [(dx, dz) for dx in (2, 1, 3, 0) for d in range(REACH, 0, -1) for dz in (d, -d)]
NEAR = [place for dx in (2, 1, 3, 0) for place in [n for n in NEAR if n[0] == dx] + [(dx, 0)]]
FAR = [(dx, dz) for dx in (2, 1, 3, 0) for dz in (8, -7, 7, -6, 6, -5, 5)]
FIRST = 28
PLACES = NEAR[:FIRST] + FAR + NEAR[FIRST:]
SPANS = [(0, 16), (16, 28), (28, 44), (44, 56), (56, 64)]
CHUNKS = len(SPANS)
SOON = 3
EARLY = SPANS[SOON][0] * MOST
Z_ORDER = [8, -7, 7, -6, 6, -5, 5, -4, 4, -3, 3, -2, 2, -1, 1, 0]
LAST = GROUPS - 1

F32, BF16 = jnp.float32, jnp.bfloat16


def iota(shape, dim):
    return lax.broadcasted_iota(jnp.int32, shape, dim)


def onehot(cond):
    return jnp.where(cond, 1.0, 0.0)


def dot(a, b):
    return lax.dot_general(a, b, (((1,), (0,)), ((), ())), preferred_element_type=F32)


def kernel(emb_in, lab_in, rank_in, out, emb, lab, rank, S, Sr, R, Rr1, Rr2, K, Q2, D2, KR, QR2, DR2, PM, PMs, BS, V,
           gate, in_s, row_s, row_r, rz_s, rz_r, rx_s, rx_r, y_s, y_r, yr_s, yr_r, pm_s, pm_r, b_s, b_r):
    dp, grp = lax.axis_index("dp"), lax.axis_index("grp")
    x, z = lax.div(dp, NZ), lax.rem(dp, NZ)
    y, core = lax.div(grp, 2), lax.rem(grp, 2)
    z_at = {dz: lax.rem(z + (dz + NZ), NZ) for dz in range(1 - NZ // 2, NZ // 2 + 1)}
    z_from = {dz: lax.rem(z + (NZ - dz), NZ) for dz in z_at}
    x_at = [lax.rem(x + dx, NX) * NZ for dx in range(NX)]
    x_from = [lax.rem(x + (NX - dx), NX) * NZ for dx in range(NX)]
    target = [x_at[dx] + z_at[dz] for dx, dz in PLACES]
    source = [x_from[dx] + z_from[dz] for dx, dz in PLACES]

    up = (dp, lax.rem(y + 1, NY) * 2 + core)
    below = lax.rem(y + (NY - 1), NY) * 2 + core
    down = (dp, below)
    sibling = (dp, y * 2 + 1 - core)
    mesh_id = pl.DeviceIdType.MESH
    started = []

    def send(src, dst, send_sem, recv_sem, to, keep=True):
        copy = pltpu.make_async_remote_copy(
            src_ref=src, dst_ref=dst, send_sem=send_sem, recv_sem=recv_sem, device_id=to, device_id_type=mesh_id
        )
        copy.start()
        if keep:
            started.append(copy)
        return copy

    def wait_all(ref, sem):
        pltpu.make_async_copy(ref, ref, sem).wait()

    barrier = pltpu.get_barrier_semaphore()
    far = [abs(dz) > REACH for _, dz in PLACES]
    peers = [(target[p], y * 2 + int(far[p])) for p in range(LAST)] + [up, down, sibling]
    for peer in peers:
        pl.semaphore_signal(barrier, inc=1, device_id=peer, device_id_type=mesh_id)

    def listen(reach, count):
        @pl.when(core == reach)
        def _():
            pl.semaphore_wait(barrier, 2 * count + 3)
            pl.semaphore_signal(gate, inc=1, device_id=sibling, device_id_type=mesh_id)

        @pl.when(core != reach)
        def _():
            pl.semaphore_wait(gate, 1)

    loads = [pltpu.make_async_copy(a, b, in_s.at[i]) for i, (a, b) in enumerate(
        ((lab_in, lab), (rank_in, rank), (emb_in, emb)))]
    for load in loads:
        load.start()
    loads[0].wait()
    loads[1].wait()

    lab_row = lab[...].astype(F32)
    i0, i1 = iota((128, 128), 0), iota((128, 128), 1)
    lab_all = jnp.broadcast_to(lab_row, (128, 128))
    lab_col = jnp.sum(jnp.where(i0 == i1, lab_all, 0.0), axis=1, keepdims=True)
    same = onehot(lab_col == lab_all)
    slot_row = jnp.sum(jnp.where(i0 < i1, same, 0.0), axis=0, keepdims=True)
    slot_col = jnp.sum(jnp.where(i1 < i0, same, 0.0), axis=1, keepdims=True)
    pos_row = lab_row * MOST + slot_row

    rank_row = rank[...].astype(F32)
    high = jnp.floor(rank_row * (1.0 / 256))
    low = rank_row - 256.0 * high
    xg_row = jnp.floor(lab_row * (1.0 / NZ))
    xg_col = jnp.floor(lab_col * (1.0 / NZ))
    mine = lab_row - NZ * xg_row == iota((NZ, 128), 0).astype(F32)
    parts = jnp.concatenate(
        [jnp.where(mine, high, 0.0), jnp.where(mine, low, 0.0), onehot(mine)], axis=0
    ).astype(BF16)
    place = onehot(xg_col * MOST + slot_col == i1.astype(F32)).astype(BF16)
    found = dot(parts, place)
    ranks = found[:NZ] * 256.0 + found[NZ:2 * NZ] + (1.0 - found[2 * NZ:]) * EMPTY
    for i in range(NZ):
        Sr[i] = ranks[i:i + 1]

    width = emb.shape[1]
    half = width // 2
    s0, s1 = iota((2 * SLOTS, 256), 0), iota((2 * SLOTS, 256), 1)
    slot_of = (s0 // 8) * MOST + s0 % MOST
    pos_two = jnp.concatenate([pos_row, pos_row], axis=1)
    spread = onehot((pos_two == slot_of.astype(F32)) & ((s0 // MOST) % 2 == s1 // 128)).astype(BF16)
    loads[2].wait()
    values = emb[...].astype(F32)
    scale = lax.rsqrt(jnp.mean(values * values, axis=1, keepdims=True) + 1e-06) / jnp.sqrt(F32(width))
    unit = (values * scale).astype(BF16)
    S[...] = dot(spread, jnp.concatenate([unit[:, :half], unit[:, half:]], axis=0)).astype(BF16).reshape(S.shape)

    chunk_of = [t for t, (lo, hi) in enumerate(SPANS) for _ in range(lo, hi)]

    def send_rows(places):
        for p in places:
            send(S.at[target[p]], R.at[p], row_s, row_r.at[chunk_of[p]], (target[p], grp), False)

    def send_ranks(distant):
        for i, dz in enumerate(Z_ORDER[:NZ - 1]):
            if (abs(dz) > REACH) == distant:
                send(Sr.at[z_at[dz]], Rr1.at[i], rz_s, rz_r, (x * NZ + z_at[dz], grp), False)

    listen(0, LAST - sum(far))
    send_rows(range(FIRST))
    send_ranks(False)
    listen(1, sum(far))
    send_ranks(True)
    send_rows(range(FIRST, LAST))
    R[LAST] = S[dp]
    Rr1[NZ - 1] = Sr[z]

    from_down, from_up, to_q2, to_d2 = {}, {}, {}, {}

    def span(t):
        lo, hi = SPANS[t]
        return lo, hi - lo, pl.ds(lo * MOST, (hi - lo) * MOST)

    def arrive(t):
        lo, places, at = span(t)
        wait_all(R.at[pl.ds(lo, places - (t == CHUNKS - 1))], row_r.at[t])
        count = places * MOST
        o0, o1 = iota((2 * count, 2 * count), 0), iota((2 * count, 2 * count), 1)
        whole = onehot(o1 == ((o0 % count) // MOST) * 8 + (o0 // count) * MOST + o0 % MOST).astype(BF16)
        rows = dot(whole, R[lo:lo + places].reshape(2 * count, half)).astype(BF16)
        K[0, lo * MOST:lo * MOST + count, :half] = rows[:count]
        K[0, lo * MOST:lo * MOST + count, half:] = rows[count:]
        from_down[t] = send(K.at[0, at], K.at[2, at], y_s.at[t, 0], y_r.at[t, 0], up)
        from_up[t] = send(K.at[0, at], K.at[1, at], y_s.at[t, 1], y_r.at[t, 1], down)
        to_q2[t] = send(K.at[0, at], Q2.at[at], y_s.at[t, 2], y_r.at[t, 2], sibling)

    def share(t):
        _, _, at = span(t)
        from_down[t].wait_recv()
        to_d2[t] = send(K.at[2, at], D2.at[at], y_s.at[t, 3], y_r.at[t, 3], sibling)

    arrive(0)
    arrive(1)
    share(0)
    share(1)

    wait_all(Rr1.at[pl.ds(0, NZ - 1)], rz_r)
    rx_copy = []
    for dx in range(1, NX):
        rx_copy.append(send(Rr1, Rr2.at[dx], rx_s.at[dx], rx_r.at[dx], (x_at[dx] + z, grp)))
    Rr2[0] = Rr1[...]
    for copy in rx_copy:
        copy.wait_recv()
    lanes = Rr2[...].reshape(GROUPS, 128)
    lane_high = jnp.floor(lanes * (1.0 / 256))
    lane_low = lanes - 256.0 * lane_high
    column = [dx * NZ + Z_ORDER.index(dz) for dx, dz in PLACES]
    r8, g1 = iota((8, GROUPS), 0), iota((8, GROUPS), 1)
    pick = jnp.concatenate(
        [onehot(g1 == jnp.where(r8 < MOST, column[p], column[p + 1])) for p in range(0, GROUPS, 2)], axis=0
    ).astype(BF16)
    both = dot(pick, jnp.concatenate([lane_high, lane_low], axis=1).astype(BF16))
    wide = both[:, :128] * 256.0 + both[:, 128:]
    w0, w1 = iota((SLOTS, 128), 0), iota((SLOTS, 128), 1)
    own_col = jnp.sum(jnp.where(w1 == x * MOST + w0 % MOST, wide, 0.0), axis=1, keepdims=True)
    d0, d1 = iota((SLOTS, SLOTS), 0), iota((SLOTS, SLOTS), 1)
    KR[0] = jnp.sum(jnp.where(d0 == d1, own_col, 0.0), axis=0, keepdims=True)
    yr_copy = [
        send(KR.at[0], KR.at[2], yr_s.at[0], yr_r.at[0], up),
        send(KR.at[0], KR.at[1], yr_s.at[1], yr_r.at[1], down),
        send(KR.at[0], QR2, yr_s.at[2], yr_r.at[2], sibling),
    ]
    for copy in yr_copy:
        copy.wait_recv()
    dr_copy = send(KR.at[2], DR2, yr_s.at[3], yr_r.at[3], sibling)

    arrive(2)
    arrive(3)
    arrive(4)

    rows8 = iota((8, 128), 0)
    cluster_of = []
    for p in range(0, GROUPS, 8):
        block = jnp.zeros((8, 128), jnp.int32)
        for i in range(8):
            block = jnp.where(rows8 == i, target[p + i], block)
        cluster_of.append(block)
    cluster_of = jnp.concatenate(cluster_of, axis=0).astype(F32)

    def cosines(best, keys, key_rank, queries, ranks_q):
        cosine = lax.dot_general(keys, queries, (((1,), (1,)), ((), ())), preferred_element_type=F32)
        masked = jnp.where(key_rank < ranks_q, cosine, -jnp.inf)
        return jnp.maximum(best, jnp.max(masked, axis=0, keepdims=True))

    dr_copy.wait_recv()
    query_rank = [KR[0], QR2[...], KR[2], DR2[...]]
    query = [K.at[0], Q2, K.at[2], D2]
    key_rank = [jnp.sum(jnp.where(d0 == d1, KR[b], 0.0), axis=1, keepdims=True) for b in range(3)]
    pairs = [(0, 0), (0, 1), (1, 0), (1, 1), (2, 0), (2, 1), (1, 2), (1, 3)]
    early = [jnp.full((1, EARLY), -1.0, F32)] * 4
    late = [jnp.full((1, SLOTS - EARLY), -1.0, F32)] * 4
    best = [jnp.full((1, SLOTS), -1.0, F32)] * 4

    for t in range(SOON):
        if t == SOON - 1:
            share(t)
        from_up[t].wait_recv()
        to_q2[t].wait_recv()
        to_d2[t].wait_recv()
    for b, c in pairs:
        early[c] = cosines(early[c], K[b, :EARLY], key_rank[b][:EARLY], query[c][:EARLY], query_rank[c][:, :EARLY])
    for t in range(SOON, CHUNKS):
        share(t)
        from_up[t].wait_recv()
        to_q2[t].wait_recv()
    for b, c in pairs:
        if c == 3:
            for t in range(SOON, CHUNKS):
                to_d2[t].wait_recv()
        late[c] = cosines(late[c], K[b, :EARLY], key_rank[b][:EARLY], query[c][EARLY:], query_rank[c][:, EARLY:])
        best[c] = cosines(best[c], K[b, EARLY:], key_rank[b][EARLY:], query[c][...], query_rank[c])
    best = [jnp.maximum(best[c], jnp.concatenate([early[c], late[c]], axis=1)) for c in range(4)]

    PMs[:, :SLOTS] = best[1]
    PMs[:, SLOTS:] = best[3]
    send(PMs, PM, pm_s, pm_r, sibling).wait_recv()
    own = jnp.maximum(best[0], PM[:, :SLOTS])
    lower = jnp.maximum(best[2], PM[:, SLOTS:])
    for i in range(2):
        BS[i] = own[:, i * 128:(i + 1) * 128]
        BS[2 + i] = lower[:, i * 128:(i + 1) * 128]

    hops = [min(dx, NX - dx) + abs(dz) for dx, dz in PLACES]
    for p in sorted(range(GROUPS), key=lambda p: -hops[p]):
        send(BS.at[2 + p // 32], V.at[GROUPS + p], b_s.at[1], b_r.at[1], (source[p], below), False)
        if p < LAST:
            send(BS.at[p // 32], V.at[p], b_s.at[0], b_r.at[0], (source[p], grp), False)
    V[LAST] = BS[1]
    a0, a1 = iota((GROUPS, 128), 0), iota((GROUPS, 128), 1)
    first = (a0 % 32) * MOST
    wait_all(V.at[pl.ds(0, LAST)], b_r.at[0])
    wait_all(V.at[pl.ds(GROUPS, GROUPS)], b_r.at[1])
    back = jnp.maximum(V[:GROUPS], V[GROUPS:]).reshape(GROUPS, 128)
    held = jnp.where((a1 >= first) & (a1 < first + MOST), back, 0.0)
    shift = 64
    while shift >= MOST:
        held = held + pltpu.roll(held, shift, 1)
        shift //= 2
    chosen = jnp.zeros((GROUPS, 128), F32)
    for s in range(MOST):
        hit = (cluster_of == lab_row) & (slot_row == float(s))
        chosen = chosen + jnp.where(hit, held[:, s:s + 1], 0.0)
    out[...] = jnp.sum(chosen, axis=0, keepdims=True)

    wait_all(R.at[pl.ds(0, LAST)], row_s)
    wait_all(Rr1.at[pl.ds(0, NZ - 1)], rz_s)
    wait_all(V.at[pl.ds(0, LAST)], b_s.at[0])
    wait_all(V.at[pl.ds(GROUPS, GROUPS)], b_s.at[1])
    for copy in started:
        copy.wait_send()


def body(embeddings, cluster, rank):
    rows, width = embeddings.shape
    sem = pltpu.SemaphoreType.DMA
    out = pl.pallas_call(
        kernel,
        out_shape=jax.ShapeDtypeStruct((1, rows), F32),
        in_specs=[pl.BlockSpec(memory_space=pl.ANY)] * 3,
        out_specs=pl.BlockSpec(memory_space=pltpu.VMEM),
        scratch_shapes=[
            pltpu.VMEM((rows, width), BF16),
            pltpu.VMEM((1, rows), jnp.int32),
            pltpu.VMEM((1, rows), jnp.int32),
            pltpu.VMEM((GROUPS, 8, width // 2), BF16),
            pltpu.VMEM((NZ, 1, 128), F32),
            pltpu.VMEM((GROUPS, 8, width // 2), BF16),
            pltpu.VMEM((NZ, 1, 128), F32),
            pltpu.VMEM((NX, NZ, 1, 128), F32),
            pltpu.VMEM((3, SLOTS, width), BF16),
            pltpu.VMEM((SLOTS, width), BF16),
            pltpu.VMEM((SLOTS, width), BF16),
            pltpu.VMEM((3, 1, SLOTS), F32),
            pltpu.VMEM((1, SLOTS), F32),
            pltpu.VMEM((1, SLOTS), F32),
            pltpu.VMEM((1, 2 * SLOTS), F32),
            pltpu.VMEM((1, 2 * SLOTS), F32),
            pltpu.VMEM((4, 1, 128), F32),
            pltpu.VMEM((2 * GROUPS, 1, 128), F32),
            pltpu.SemaphoreType.REGULAR,
            sem((3,)),
            sem, sem((CHUNKS,)), sem, sem, sem((NX,)), sem((NX,)),
            sem((CHUNKS, 4)), sem((CHUNKS, 4)), sem((4,)), sem((4,)),
            sem, sem, sem((2,)), sem((2,)),
        ],
        compiler_params=pltpu.CompilerParams(
            collective_id=0, has_side_effects=True, vmem_limit_bytes=40 * 1024 * 1024
        ),
    )(embeddings, cluster.reshape(1, rows), rank.reshape(1, rows))
    return out.reshape(rows)


def solution(mesh):
    in_specs = (P(("dp", "grp"), None), P(("dp", "grp"), None), P(("dp", "grp")))
    out_specs = P(("dp", "grp"))
    return jax.shard_map(body, mesh=mesh, in_specs=in_specs, out_specs=out_specs, check_vma=False)
```

time: 61.5 us -> 57.1 us (0.928)
  Pallas kernels: 59.2 us -> 54.8 us
    pallas_call x1, Pallas kernels: 59.2 us -> 54.8 us  [body(): pl.pallas_call(kernel, out_shape=jax.ShapeDtypeStruct((1, rows), F32), in...]
where the time goes in v4:
time: 57.1 us; the launch traced here: 56.9 us
  Pallas kernels  54.8 us (96%)
  local copies, waits for them, and re-layouts  2.11 us (4%)
    pallas_call x1, Pallas kernels, body(): pl.pallas_call(kernel, out_shape=jax.ShapeDtypeStruct((1, rows), F32), in...  54.8 us
    unnamed x7, local copies, waits for them, and re-layouts  2.11 us

profile of v4, /device:TPU:1, one launch (start us, length us, event | category | flops | bytes accessed | tf_op | source)
XLA Modules:
  0.0 56.9 jit_solution(11639178869262292290)
XLA Ops:
  0.0 0.0 copy-start.1
  0.0 0.0 copy-start.2
  0.0 0.7 %copy-done.1 = s32[128,1]{0,1:T(1,128)S(1)} copy-done((s32[128,1]{0,1:T(1,128)S(1)}, s32[128,1]{0,1:T(1,128)}, u32[]{:S(2)}) %copy-start.1) | copy-done | bytes 536
  0.7 0.0 copy-done.2
  0.7 0.0 copy-start
  0.7 0.9 %copy-done = bf16[128,768]{1,0:T(8,128)(2,1)S(1)} copy-done((bf16[128,768]{1,0:T(8,128)(2,1)S(1)}, bf16[128,768]{1,0:T(8,128)(2,1)}, u32[]{:S(2)}) %copy-start) | copy-done | bytes 196632
  1.6 54.8 %shard_map.37 = f32[1,128]{1,0:T(1,128)S(1)} custom-call(bf16[128,768]{1,0:T(8,128)(2,1)S(1)} %copy-done, s32[1,128]{1,0:T(1,128)S(1)} %bitcast.3, s32[1,128]{1,0:T(1,128)S(1)} %bitcast.4), custom_call_target="tpu_custom_call" | custom-call | tf_op jit(solution)/shard_map/pallas_call | solution.py:300
  56.4 0.5 copy.5
Async XLA Ops:
  0.0 0.7 %copy-start.1 = (s32[128,1]{0,1:T(1,128)S(1)}, s32[128,1]{0,1:T(1,128)}, u32[]{:S(2)}) copy-start(s32[128,1]{0,1:T(1,128)} %param.4) | copy-start | bytes 1540
  0.0 0.7 %copy-start.2 = (s32[128]{0:T(128)S(1)}, s32[128]{0:T(128)}, u32[]{:S(2)}) copy-start(s32[128]{0:T(128)} %param.5) | copy-start | bytes 1540
  0.7 0.9 %copy-start = (bf16[128,768]{1,0:T(8,128)(2,1)S(1)}, bf16[128,768]{1,0:T(8,128)(2,1)}, u32[]{:S(2)}) copy-start(bf16[128,768]{1,0:T(8,128)(2,1)} %emb_in.1) | copy-start | bytes 589828

commit v5 on v4

--- a/solution.py
+++ b/solution.py
@@ -11,18 +11,17 @@
 SLOTS = GROUPS * MOST
 EMPTY = 65536.0
 
+LAST = GROUPS - 1
 REACH = 4
-NEAR = [(dx, dz) for dx in (2, 1, 3, 0) for d in range(REACH, 0, -1) for dz in (d, -d)]
-NEAR = [place for dx in (2, 1, 3, 0) for place in [n for n in NEAR if n[0] == dx] + [(dx, 0)]]
-FAR = [(dx, dz) for dx in (2, 1, 3, 0) for dz in (8, -7, 7, -6, 6, -5, 5)]
-FIRST = 28
-PLACES = NEAR[:FIRST] + FAR + NEAR[FIRST:]
-SPANS = [(0, 16), (16, 28), (28, 44), (44, 56), (56, 64)]
+DZ_NEAR = [4, -4, 3, -3, 2, -2, 1, -1, 0]
+DZ_FAR = [8, -7, 7, -6, 6, -5, 5]
+NEAR = [(dx, dz) for dx in (2, 1, 3, 0) for dz in DZ_NEAR][:-1]
+PLACES = NEAR + [(dx, dz) for dx in (2, 1, 3, 0) for dz in DZ_FAR] + [(0, 0)]
+FIRST = len(NEAR)
+SPANS = [(0, 16), (16, 32), (32, 40), (40, 48), (48, 56), (56, 64)]
+WINDOWS = [(0, FIRST), (FIRST, 40), (40, 48), (48, 56), (56, LAST)]
 CHUNKS = len(SPANS)
-SOON = 3
-EARLY = SPANS[SOON][0] * MOST
 Z_ORDER = [8, -7, 7, -6, 6, -5, 5, -4, 4, -3, 3, -2, 2, -1, 1, 0]
-LAST = GROUPS - 1
 
 F32, BF16 = jnp.float32, jnp.bfloat16
 
@@ -131,9 +130,15 @@
 
     chunk_of = [t for t, (lo, hi) in enumerate(SPANS) for _ in range(lo, hi)]
 
+    window_of = [w for w, (lo, hi) in enumerate(WINDOWS) for _ in range(lo, hi)]
+
+    def sent(w):
+        lo, hi = WINDOWS[w]
+        wait_all(R.at[pl.ds(lo, hi - lo)], row_s.at[w])
+
     def send_rows(places):
         for p in places:
-            send(S.at[target[p]], R.at[p], row_s, row_r.at[chunk_of[p]], (target[p], grp), False)
+            send(S.at[target[p]], R.at[p], row_s.at[window_of[p]], row_r.at[chunk_of[p]], (target[p], grp), False)
 
     def send_ranks(distant):
         for i, dz in enumerate(Z_ORDER[:NZ - 1]):
@@ -145,7 +150,7 @@
     send_ranks(False)
     listen(1, sum(far))
     send_ranks(True)
-    send_rows(range(FIRST, LAST))
+    send_rows(range(FIRST, 48))
     R[LAST] = S[dp]
     Rr1[NZ - 1] = Sr[z]
 
@@ -174,15 +179,20 @@
         to_d2[t] = send(K.at[2, at], D2.at[at], y_s.at[t, 3], y_r.at[t, 3], sibling)
 
     arrive(0)
+    sent(1)
+    send_rows(range(48, 56))
     arrive(1)
-    share(0)
-    share(1)
+    sent(2)
+    send_rows(range(56, LAST))
 
     wait_all(Rr1.at[pl.ds(0, NZ - 1)], rz_r)
     rx_copy = []
     for dx in range(1, NX):
         rx_copy.append(send(Rr1, Rr2.at[dx], rx_s.at[dx], rx_r.at[dx], (x_at[dx] + z, grp)))
     Rr2[0] = Rr1[...]
+    share(0)
+    share(1)
+    arrive(2)
     for copy in rx_copy:
         copy.wait_recv()
     lanes = Rr2[...].reshape(GROUPS, 128)
@@ -204,14 +214,8 @@
         send(KR.at[0], KR.at[1], yr_s.at[1], yr_r.at[1], down),
         send(KR.at[0], QR2, yr_s.at[2], yr_r.at[2], sibling),
     ]
-    for copy in yr_copy:
-        copy.wait_recv()
-    dr_copy = send(KR.at[2], DR2, yr_s.at[3], yr_r.at[3], sibling)
-
-    arrive(2)
+
     arrive(3)
-    arrive(4)
-
     rows8 = iota((8, 128), 0)
     cluster_of = []
     for p in range(0, GROUPS, 8):
@@ -221,52 +225,52 @@
         cluster_of.append(block)
     cluster_of = jnp.concatenate(cluster_of, axis=0).astype(F32)
 
-    def cosines(best, keys, key_rank, queries, ranks_q):
-        cosine = lax.dot_general(keys, queries, (((1,), (1,)), ((), ())), preferred_element_type=F32)
-        masked = jnp.where(key_rank < ranks_q, cosine, -jnp.inf)
-        return jnp.maximum(best, jnp.max(masked, axis=0, keepdims=True))
-
+    arrive(4)
+    for copy in yr_copy:
+        copy.wait_recv()
+    dr_copy = send(KR.at[2], DR2, yr_s.at[3], yr_r.at[3], sibling)
+    key_rank = [jnp.sum(jnp.where(d0 == d1, KR[b], 0.0), axis=1, keepdims=True) for b in range(3)]
+    arrive(5)
+    for t in range(2, CHUNKS):
+        share(t)
     dr_copy.wait_recv()
     query_rank = [KR[0], QR2[...], KR[2], DR2[...]]
     query = [K.at[0], Q2, K.at[2], D2]
-    key_rank = [jnp.sum(jnp.where(d0 == d1, KR[b], 0.0), axis=1, keepdims=True) for b in range(3)]
-    pairs = [(0, 0), (0, 1), (1, 0), (1, 1), (2, 0), (2, 1), (1, 2), (1, 3)]
-    early = [jnp.full((1, EARLY), -1.0, F32)] * 4
-    late = [jnp.full((1, SLOTS - EARLY), -1.0, F32)] * 4
-    best = [jnp.full((1, SLOTS), -1.0, F32)] * 4
-
-    for t in range(SOON):
-        if t == SOON - 1:
-            share(t)
+
+    def largest(c, chips):
+        best = jnp.full((1, SLOTS), -1.0, F32)
+        for b in chips:
+            cosine = lax.dot_general(K[b], query[c][...], (((1,), (1,)), ((), ())), preferred_element_type=F32)
+            masked = jnp.where(key_rank[b] < query_rank[c], cosine, -jnp.inf)
+            best = jnp.maximum(best, jnp.max(masked, axis=0, keepdims=True))
+        return best
+
+    for t in range(CHUNKS):
         from_up[t].wait_recv()
+    lower = largest(2, (1,))
+    for t in range(CHUNKS):
+        to_d2[t].wait_recv()
+    PMs[1] = largest(3, (1,))
+    pm_lower = send(PMs.at[1], PM.at[1], pm_s.at[1], pm_r.at[1], sibling)
+    for t in range(CHUNKS):
         to_q2[t].wait_recv()
-        to_d2[t].wait_recv()
-    for b, c in pairs:
-        early[c] = cosines(early[c], K[b, :EARLY], key_rank[b][:EARLY], query[c][:EARLY], query_rank[c][:, :EARLY])
-    for t in range(SOON, CHUNKS):
-        share(t)
-        from_up[t].wait_recv()
-        to_q2[t].wait_recv()
-    for b, c in pairs:
-        if c == 3:
-            for t in range(SOON, CHUNKS):
-                to_d2[t].wait_recv()
-        late[c] = cosines(late[c], K[b, :EARLY], key_rank[b][:EARLY], query[c][EARLY:], query_rank[c][:, EARLY:])
-        best[c] = cosines(best[c], K[b, EARLY:], key_rank[b][EARLY:], query[c][...], query_rank[c])
-    best = [jnp.maximum(best[c], jnp.concatenate([early[c], late[c]], axis=1)) for c in range(4)]
-
-    PMs[:, :SLOTS] = best[1]
-    PMs[:, SLOTS:] = best[3]
-    send(PMs, PM, pm_s, pm_r, sibling).wait_recv()
-    own = jnp.maximum(best[0], PM[:, :SLOTS])
-    lower = jnp.maximum(best[2], PM[:, SLOTS:])
+    PMs[0] = largest(1, range(3))
+    pm_own = send(PMs.at[0], PM.at[0], pm_s.at[0], pm_r.at[0], sibling)
+    own = largest(0, range(3))
+
+    hops = [min(dx, NX - dx) + abs(dz) for dx, dz in PLACES]
+    far_first = sorted(range(GROUPS), key=lambda p: -hops[p])
+    pm_lower.wait_recv()
+    lower = jnp.maximum(lower, PM[1])
+    for i in range(2):
+        BS[2 + i] = lower[:, i * 128:(i + 1) * 128]
+    for p in far_first:
+        send(BS.at[2 + p // 32], V.at[GROUPS + p], b_s.at[1], b_r.at[1], (source[p], below), False)
+    pm_own.wait_recv()
+    own = jnp.maximum(own, PM[0])
     for i in range(2):
         BS[i] = own[:, i * 128:(i + 1) * 128]
-        BS[2 + i] = lower[:, i * 128:(i + 1) * 128]
-
-    hops = [min(dx, NX - dx) + abs(dz) for dx, dz in PLACES]
-    for p in sorted(range(GROUPS), key=lambda p: -hops[p]):
-        send(BS.at[2 + p // 32], V.at[GROUPS + p], b_s.at[1], b_r.at[1], (source[p], below), False)
+    for p in far_first:
         if p < LAST:
             send(BS.at[p // 32], V.at[p], b_s.at[0], b_r.at[0], (source[p], grp), False)
     V[LAST] = BS[1]
@@ -286,7 +290,8 @@
         chosen = chosen + jnp.where(hit, held[:, s:s + 1], 0.0)
     out[...] = jnp.sum(chosen, axis=0, keepdims=True)
 
-    wait_all(R.at[pl.ds(0, LAST)], row_s)
+    for w in (0, 3, 4):
+        sent(w)
     wait_all(Rr1.at[pl.ds(0, NZ - 1)], rz_s)
     wait_all(V.at[pl.ds(0, LAST)], b_s.at[0])
     wait_all(V.at[pl.ds(GROUPS, GROUPS)], b_s.at[1])
@@ -300,7 +305,7 @@
     out = pl.pallas_call(
         kernel,
         out_shape=jax.ShapeDtypeStruct((1, rows), F32),
-        in_specs=[pl.BlockSpec(memory_space=pl.ANY)] * 3,
+        in_specs=[pl.BlockSpec(memory_space=pltpu.HBM)] * 3,
         out_specs=pl.BlockSpec(memory_space=pltpu.VMEM),
         scratch_shapes=[
             pltpu.VMEM((rows, width), BF16),
@@ -317,20 +322,20 @@
             pltpu.VMEM((3, 1, SLOTS), F32),
             pltpu.VMEM((1, SLOTS), F32),
             pltpu.VMEM((1, SLOTS), F32),
-            pltpu.VMEM((1, 2 * SLOTS), F32),
-            pltpu.VMEM((1, 2 * SLOTS), F32),
+            pltpu.VMEM((2, 1, SLOTS), F32),
+            pltpu.VMEM((2, 1, SLOTS), F32),
             pltpu.VMEM((4, 1, 128), F32),
             pltpu.VMEM((2 * GROUPS, 1, 128), F32),
             pltpu.SemaphoreType.REGULAR,
             sem((3,)),
-            sem, sem((CHUNKS,)), sem, sem, sem((NX,)), sem((NX,)),
+            sem((len(WINDOWS),)), sem((CHUNKS,)), sem, sem, sem((NX,)), sem((NX,)),
             sem((CHUNKS, 4)), sem((CHUNKS, 4)), sem((4,)), sem((4,)),
-            sem, sem, sem((2,)), sem((2,)),
+            sem((2,)), sem((2,)), sem((2,)), sem((2,)),
         ],
         compiler_params=pltpu.CompilerParams(
             collective_id=0, has_side_effects=True, vmem_limit_bytes=40 * 1024 * 1024
         ),
-    )(embeddings, cluster.reshape(1, rows), rank.reshape(1, rows))
+    )(*(pltpu.with_memory_space_constraint(a, pltpu.HBM) for a in (embeddings, cluster.reshape(1, rows), rank.reshape(1, rows))))
     return out.reshape(rows)
 
 

time: 57.1 us -> 55 us (0.963)
  local copies, waits for them, and re-layouts: 2.11 us -> 0.51 us
    unnamed x7 -> x1, local copies, waits for them, and re-layouts: 2.11 us -> 0.51 us
where the time goes in v5:
time: 55 us; the launch traced here: 54.9 us
  Pallas kernels  54.4 us (99%)
    pallas_call x1, Pallas kernels, body(): pl.pallas_call(kernel, out_shape=jax.ShapeDtypeStruct((1, rows), F32), in...  54.4 us

profile of v5, /device:TPU:1, one launch (start us, length us, event | category | flops | bytes accessed | tf_op | source)
XLA Modules:
  0.0 54.9 jit_solution(385424235488276039)
XLA Ops:
  0.0 54.4 %shard_map.37 = f32[1,128]{1,0:T(1,128)S(1)} custom-call(bf16[128,768]{1,0:T(8,128)(2,1)} %emb_in.1, s32[1,128]{1,0:T(1,128)} %bitcast.4, s32[1,128]{1,0:T(1,128)} %bitcast.5), custom_call_target="tpu_custom_call" | custom-call | tf_op jit(solution)/shard_map/pallas_call | solution.py:305
  54.4 0.5 copy.5

commit v6 on v5

--- a/solution.py
+++ b/solution.py
@@ -11,7 +11,6 @@
 SLOTS = GROUPS * MOST
 EMPTY = 65536.0
 
-LAST = GROUPS - 1
 REACH = 4
 DZ_NEAR = [4, -4, 3, -3, 2, -2, 1, -1, 0]
 DZ_FAR = [8, -7, 7, -6, 6, -5, 5]
@@ -19,9 +18,9 @@
 PLACES = NEAR + [(dx, dz) for dx in (2, 1, 3, 0) for dz in DZ_FAR] + [(0, 0)]
 FIRST = len(NEAR)
 SPANS = [(0, 16), (16, 32), (32, 40), (40, 48), (48, 56), (56, 64)]
-WINDOWS = [(0, FIRST), (FIRST, 40), (40, 48), (48, 56), (56, LAST)]
 CHUNKS = len(SPANS)
 Z_ORDER = [8, -7, 7, -6, 6, -5, 5, -4, 4, -3, 3, -2, 2, -1, 1, 0]
+LAST = GROUPS - 1
 
 F32, BF16 = jnp.float32, jnp.bfloat16
 
@@ -72,6 +71,8 @@
     barrier = pltpu.get_barrier_semaphore()
     far = [abs(dz) > REACH for _, dz in PLACES]
     peers = [(target[p], y * 2 + int(far[p])) for p in range(LAST)] + [up, down, sibling]
+    distance = [min(dx, NX - dx) + abs(dz) for dx, dz in PLACES]
+    peers[:LAST] = [peers[p] for p in sorted(range(LAST), key=lambda p: -distance[p])]
     for peer in peers:
         pl.semaphore_signal(barrier, inc=1, device_id=peer, device_id_type=mesh_id)
 
@@ -130,15 +131,9 @@
 
     chunk_of = [t for t, (lo, hi) in enumerate(SPANS) for _ in range(lo, hi)]
 
-    window_of = [w for w, (lo, hi) in enumerate(WINDOWS) for _ in range(lo, hi)]
-
-    def sent(w):
-        lo, hi = WINDOWS[w]
-        wait_all(R.at[pl.ds(lo, hi - lo)], row_s.at[w])
-
     def send_rows(places):
         for p in places:
-            send(S.at[target[p]], R.at[p], row_s.at[window_of[p]], row_r.at[chunk_of[p]], (target[p], grp), False)
+            send(S.at[target[p]], R.at[p], row_s, row_r.at[chunk_of[p]], (target[p], grp), False)
 
     def send_ranks(distant):
         for i, dz in enumerate(Z_ORDER[:NZ - 1]):
@@ -150,7 +145,7 @@
     send_ranks(False)
     listen(1, sum(far))
     send_ranks(True)
-    send_rows(range(FIRST, 48))
+    send_rows(range(FIRST, LAST))
     R[LAST] = S[dp]
     Rr1[NZ - 1] = Sr[z]
 
@@ -179,11 +174,7 @@
         to_d2[t] = send(K.at[2, at], D2.at[at], y_s.at[t, 3], y_r.at[t, 3], sibling)
 
     arrive(0)
-    sent(1)
-    send_rows(range(48, 56))
     arrive(1)
-    sent(2)
-    send_rows(range(56, LAST))
 
     wait_all(Rr1.at[pl.ds(0, NZ - 1)], rz_r)
     rx_copy = []
@@ -247,61 +238,68 @@
 
     for t in range(CHUNKS):
         from_up[t].wait_recv()
+        to_q2[t].wait_recv()
+    PMs[0] = largest(1, range(3))
+    pm_own = send(PMs.at[0], PM.at[0], pm_s.at[0], pm_r.at[0], sibling)
+    own = largest(0, range(3))
     lower = largest(2, (1,))
     for t in range(CHUNKS):
         to_d2[t].wait_recv()
     PMs[1] = largest(3, (1,))
     pm_lower = send(PMs.at[1], PM.at[1], pm_s.at[1], pm_r.at[1], sibling)
-    for t in range(CHUNKS):
-        to_q2[t].wait_recv()
-    PMs[0] = largest(1, range(3))
-    pm_own = send(PMs.at[0], PM.at[0], pm_s.at[0], pm_r.at[0], sibling)
-    own = largest(0, range(3))
 
     hops = [min(dx, NX - dx) + abs(dz) for dx, dz in PLACES]
     far_first = sorted(range(GROUPS), key=lambda p: -hops[p])
+
+    def send_back(places):
+        for p in places:
+            if p < LAST:
+                send(BS.at[p // 32], V.at[p], b_s.at[0], b_r.at[0], (source[p], grp), False)
+
+    pm_own.wait_recv()
+    own = jnp.maximum(own, PM[0])
+    for i in range(2):
+        BS[i] = own[:, i * 128:(i + 1) * 128]
+    send_back(far_first[:24])
     pm_lower.wait_recv()
     lower = jnp.maximum(lower, PM[1])
     for i in range(2):
         BS[2 + i] = lower[:, i * 128:(i + 1) * 128]
     for p in far_first:
         send(BS.at[2 + p // 32], V.at[GROUPS + p], b_s.at[1], b_r.at[1], (source[p], below), False)
-    pm_own.wait_recv()
-    own = jnp.maximum(own, PM[0])
-    for i in range(2):
-        BS[i] = own[:, i * 128:(i + 1) * 128]
-    for p in far_first:
-        if p < LAST:
-            send(BS.at[p // 32], V.at[p], b_s.at[0], b_r.at[0], (source[p], grp), False)
+    send_back(far_first[24:])
     V[LAST] = BS[1]
     a0, a1 = iota((GROUPS, 128), 0), iota((GROUPS, 128), 1)
     first = (a0 % 32) * MOST
+    hits = [(cluster_of == lab_row) & (slot_row == float(s)) for s in range(MOST)]
+    mine = (a1 >= first) & (a1 < first + MOST)
+
+    wait_all(R.at[pl.ds(0, LAST)], row_s)
+    wait_all(Rr1.at[pl.ds(0, NZ - 1)], rz_s)
+    wait_all(V.at[pl.ds(0, LAST)], b_s.at[0])
+    wait_all(V.at[pl.ds(GROUPS, GROUPS)], b_s.at[1])
+    for copy in started:
+        copy.wait_send()
+
     wait_all(V.at[pl.ds(0, LAST)], b_r.at[0])
     wait_all(V.at[pl.ds(GROUPS, GROUPS)], b_r.at[1])
     back = jnp.maximum(V[:GROUPS], V[GROUPS:]).reshape(GROUPS, 128)
-    held = jnp.where((a1 >= first) & (a1 < first + MOST), back, 0.0)
+    held = jnp.where(mine, back, 0.0)
     shift = 64
     while shift >= MOST:
         held = held + pltpu.roll(held, shift, 1)
         shift //= 2
     chosen = jnp.zeros((GROUPS, 128), F32)
     for s in range(MOST):
-        hit = (cluster_of == lab_row) & (slot_row == float(s))
-        chosen = chosen + jnp.where(hit, held[:, s:s + 1], 0.0)
+        chosen = chosen + jnp.where(hits[s], held[:, s:s + 1], 0.0)
     out[...] = jnp.sum(chosen, axis=0, keepdims=True)
-
-    for w in (0, 3, 4):
-        sent(w)
-    wait_all(Rr1.at[pl.ds(0, NZ - 1)], rz_s)
-    wait_all(V.at[pl.ds(0, LAST)], b_s.at[0])
-    wait_all(V.at[pl.ds(GROUPS, GROUPS)], b_s.at[1])
-    for copy in started:
-        copy.wait_send()
 
 
 def body(embeddings, cluster, rank):
     rows, width = embeddings.shape
     sem = pltpu.SemaphoreType.DMA
+    operands = [embeddings, cluster.reshape(1, rows), rank.reshape(1, rows)]
+    operands = [pltpu.with_memory_space_constraint(operand, pltpu.HBM) for operand in operands]
     out = pl.pallas_call(
         kernel,
         out_shape=jax.ShapeDtypeStruct((1, rows), F32),
@@ -328,14 +326,14 @@
             pltpu.VMEM((2 * GROUPS, 1, 128), F32),
             pltpu.SemaphoreType.REGULAR,
             sem((3,)),
-            sem((len(WINDOWS),)), sem((CHUNKS,)), sem, sem, sem((NX,)), sem((NX,)),
+            sem, sem((CHUNKS,)), sem, sem, sem((NX,)), sem((NX,)),
             sem((CHUNKS, 4)), sem((CHUNKS, 4)), sem((4,)), sem((4,)),
             sem((2,)), sem((2,)), sem((2,)), sem((2,)),
         ],
         compiler_params=pltpu.CompilerParams(
             collective_id=0, has_side_effects=True, vmem_limit_bytes=40 * 1024 * 1024
         ),
-    )(*(pltpu.with_memory_space_constraint(a, pltpu.HBM) for a in (embeddings, cluster.reshape(1, rows), rank.reshape(1, rows))))
+    )(*operands)
     return out.reshape(rows)
 
 

time: 55 us -> 54.5 us (level)
  Pallas kernels: 54.4 us -> 53.8 us
where the time goes in v6:
time: 54.5 us; the launch traced here: 54.3 us
  Pallas kernels  53.8 us (99%)
    pallas_call x1, Pallas kernels, body(): pl.pallas_call(kernel, out_shape=jax.ShapeDtypeStruct((1, rows), F32), in...  53.8 us

profile of v6, /device:TPU:1, one launch (start us, length us, event | category | flops | bytes accessed | tf_op | source)
XLA Modules:
  0.0 54.3 jit_solution(4211125679700410697)
XLA Ops:
  0.0 53.8 %shard_map.37 = f32[1,128]{1,0:T(1,128)S(1)} custom-call(bf16[128,768]{1,0:T(8,128)(2,1)} %emb_in.1, s32[1,128]{1,0:T(1,128)} %bitcast.4, s32[1,128]{1,0:T(1,128)} %bitcast.5), custom_call_target="tpu_custom_call" | custom-call | tf_op jit(solution)/shard_map/pallas_call | solution.py:303
  53.8 0.5 copy.5

commit v7 on v6

--- a/solution.py
+++ b/solution.py
@@ -21,6 +21,7 @@
 CHUNKS = len(SPANS)
 Z_ORDER = [8, -7, 7, -6, 6, -5, 5, -4, 4, -3, 3, -2, 2, -1, 1, 0]
 LAST = GROUPS - 1
+WINDOWS = [(0, FIRST), (FIRST, 40), (40, 48), (48, 56), (56, LAST)]
 
 F32, BF16 = jnp.float32, jnp.bfloat16
 
@@ -131,9 +132,15 @@
 
     chunk_of = [t for t, (lo, hi) in enumerate(SPANS) for _ in range(lo, hi)]
 
+    window_of = [w for w, (lo, hi) in enumerate(WINDOWS) for _ in range(lo, hi)]
+
+    def sent(w):
+        lo, hi = WINDOWS[w]
+        wait_all(R.at[pl.ds(lo, hi - lo)], row_s.at[w])
+
     def send_rows(places):
         for p in places:
-            send(S.at[target[p]], R.at[p], row_s, row_r.at[chunk_of[p]], (target[p], grp), False)
+            send(S.at[target[p]], R.at[p], row_s.at[window_of[p]], row_r.at[chunk_of[p]], (target[p], grp), False)
 
     def send_ranks(distant):
         for i, dz in enumerate(Z_ORDER[:NZ - 1]):
@@ -145,7 +152,7 @@
     send_ranks(False)
     listen(1, sum(far))
     send_ranks(True)
-    send_rows(range(FIRST, LAST))
+    send_rows(range(FIRST, 48))
     R[LAST] = S[dp]
     Rr1[NZ - 1] = Sr[z]
 
@@ -174,7 +181,11 @@
         to_d2[t] = send(K.at[2, at], D2.at[at], y_s.at[t, 3], y_r.at[t, 3], sibling)
 
     arrive(0)
+    sent(1)
+    send_rows(range(48, 56))
     arrive(1)
+    sent(2)
+    send_rows(range(56, LAST))
 
     wait_all(Rr1.at[pl.ds(0, NZ - 1)], rz_r)
     rx_copy = []
@@ -274,7 +285,8 @@
     hits = [(cluster_of == lab_row) & (slot_row == float(s)) for s in range(MOST)]
     mine = (a1 >= first) & (a1 < first + MOST)
 
-    wait_all(R.at[pl.ds(0, LAST)], row_s)
+    for w in (0, 3, 4):
+        sent(w)
     wait_all(Rr1.at[pl.ds(0, NZ - 1)], rz_s)
     wait_all(V.at[pl.ds(0, LAST)], b_s.at[0])
     wait_all(V.at[pl.ds(GROUPS, GROUPS)], b_s.at[1])
@@ -326,7 +338,7 @@
             pltpu.VMEM((2 * GROUPS, 1, 128), F32),
             pltpu.SemaphoreType.REGULAR,
             sem((3,)),
-            sem, sem((CHUNKS,)), sem, sem, sem((NX,)), sem((NX,)),
+            sem((len(WINDOWS),)), sem((CHUNKS,)), sem, sem, sem((NX,)), sem((NX,)),
             sem((CHUNKS, 4)), sem((CHUNKS, 4)), sem((4,)), sem((4,)),
             sem((2,)), sem((2,)), sem((2,)), sem((2,)),
         ],

time: 54.5 us -> 54.4 us (level)
  no operation moved by 1% of the time
where the time goes in v7:
time: 54.4 us; the launch traced here: 54.3 us
  Pallas kernels  53.8 us (99%)
    pallas_call x1, Pallas kernels, body(): pl.pallas_call(kernel, out_shape=jax.ShapeDtypeStruct((1, rows), F32), in...  53.8 us

profile of v7, /device:TPU:1, one launch (start us, length us, event | category | flops | bytes accessed | tf_op | source)
XLA Modules:
  0.0 54.3 jit_solution(9168338056169106978)
XLA Ops:
  0.0 53.8 %shard_map.37 = f32[1,128]{1,0:T(1,128)S(1)} custom-call(bf16[128,768]{1,0:T(8,128)(2,1)} %emb_in.1, s32[1,128]{1,0:T(1,128)} %bitcast.4, s32[1,128]{1,0:T(1,128)} %bitcast.5), custom_call_target="tpu_custom_call" | custom-call | tf_op jit(solution)/shard_map/pallas_call | solution.py:315
  53.8 0.5 copy.5

commit v8 on v6

--- a/solution.py
+++ b/solution.py
@@ -17,7 +17,7 @@
 NEAR = [(dx, dz) for dx in (2, 1, 3, 0) for dz in DZ_NEAR][:-1]
 PLACES = NEAR + [(dx, dz) for dx in (2, 1, 3, 0) for dz in DZ_FAR] + [(0, 0)]
 FIRST = len(NEAR)
-SPANS = [(0, 16), (16, 32), (32, 40), (40, 48), (48, 56), (56, 64)]
+SPANS = [(0, 16), (16, 32), (32, 40), (40, 48), (48, 56), (56, 60), (60, 64)]
 CHUNKS = len(SPANS)
 Z_ORDER = [8, -7, 7, -6, 6, -5, 5, -4, 4, -3, 3, -2, 2, -1, 1, 0]
 LAST = GROUPS - 1
@@ -222,6 +222,7 @@
     dr_copy = send(KR.at[2], DR2, yr_s.at[3], yr_r.at[3], sibling)
     key_rank = [jnp.sum(jnp.where(d0 == d1, KR[b], 0.0), axis=1, keepdims=True) for b in range(3)]
     arrive(5)
+    arrive(6)
     for t in range(2, CHUNKS):
         share(t)
     dr_copy.wait_recv()

time: 54.5 us -> 54.5 us (level)
  no operation moved by 1% of the time
where the time goes in v8:
time: 54.5 us; the launch traced here: 54.4 us
  Pallas kernels  53.9 us (99%)
    pallas_call x1, Pallas kernels, body(): pl.pallas_call(kernel, out_shape=jax.ShapeDtypeStruct((1, rows), F32), in...  53.9 us

profile of v8, /device:TPU:1, one launch (start us, length us, event | category | flops | bytes accessed | tf_op | source)
XLA Modules:
  0.0 54.4 jit_solution(14139748766219175954)
XLA Ops:
  0.0 53.9 %shard_map.37 = f32[1,128]{1,0:T(1,128)S(1)} custom-call(bf16[128,768]{1,0:T(8,128)(2,1)} %emb_in.1, s32[1,128]{1,0:T(1,128)} %bitcast.4, s32[1,128]{1,0:T(1,128)} %bitcast.5), custom_call_target="tpu_custom_call" | custom-call | tf_op jit(solution)/shard_map/pallas_call | solution.py:304
  53.9 0.5 copy.5
